TPU v7x, 32 devices: a whole 2x2x4 slice. The times are simulated.
32 devices in a mesh: row: 8 (over y, x, core), col: 4 (over z).
Axes of the slice: x: 2, y: 2, z: 4, core: 2. Of those that a mesh axis runs over, the one named last changes fastest.
Arguments:
- spectra: bfloat16 [32, 4096, 512], P(None, ('row', 'col')), may hold values from -6 to 6
- quality: int32 [4096], P(('row', 'col')), may hold values 0 or 1
- tile_mask: int32 [32, 32], replicated, may hold values 0 or 1
Outputs:
- correlations: bfloat16 [64, 4096, 4096], P(None, 'row', 'col')
All inputs are finite; a program needn't handle non-finite values. No bound on the sum of `quality` on one device may be relied on, other than what follows from the above.
Results may differ from a plain program's by a relative error of at most 0.0066.
Values may be sent and summed in bfloat16 or wider, within the bound.
No kernel may reach another device: no remote copies, remote signals or barrier semaphores. Data moves between devices by JAX's collectives and lax.ppermute only.
A program may use at most 256 MiB of HBM per device.

v0:
```python
import math

import jax
import jax.numpy as jnp
from jax import lax
from jax.sharding import PartitionSpec as P

F = 32
LAGS = 64
W = 256
BLK = 128


def whiten(spectra, quality):
    values = spectra.astype(jnp.float32)
    half_width = values.shape[2] // 2
    real_part = values[:, :, :half_width]
    imag_part = values[:, :, half_width:]
    energy = real_part * real_part + imag_part * imag_part
    mean_energy = jnp.mean(energy, axis=0, keepdims=True)
    factor = quality.astype(jnp.float32)[None, :, None] / jnp.sqrt(energy + mean_energy + 1e-06)
    return jnp.concatenate([real_part * factor, imag_part * factor], axis=2).astype(jnp.bfloat16)


def make_basis():
    lag_offset = jnp.arange(LAGS, dtype=jnp.float32) - LAGS / 2
    frequency = jnp.arange(F, dtype=jnp.float32) + 1.0
    angles = 2.0 * math.pi * frequency[None, :] * lag_offset[:, None] / (2.0 * LAGS)
    return jnp.stack([jnp.cos(angles), -jnp.sin(angles)], axis=1).astype(jnp.bfloat16)


def per_device(spectra, quality, tile_mask):
    white = whiten(spectra, quality)
    row_block = lax.all_gather(white, "col", axis=1, tiled=True)
    col_index = lax.axis_index("col")
    row_index = lax.axis_index("row")
    values = row_block.astype(jnp.float32)
    zeros_like = jnp.zeros_like(values)
    lower_term = jnp.where(row_index == 2 * col_index, values, zeros_like)
    upper_term = jnp.where(row_index == 2 * col_index + 1, values, zeros_like)
    sectioned = jnp.concatenate([lower_term, upper_term], axis=1)
    share = lax.psum_scatter(sectioned.astype(jnp.bfloat16), "row", scatter_dimension=1, tiled=True)
    col_block = lax.all_gather(share, "row", axis=1, tiled=True)
    half_width = col_block.shape[2] // 2
    turned = jnp.concatenate([-col_block[:, :, half_width:], col_block[:, :, :half_width]], axis=2)
    both_parts = jnp.concatenate([col_block, turned], axis=1)
    row_count = row_block.shape[1]
    col_count = col_block.shape[1]
    blocks = row_count // BLK
    col_tiles = col_count // BLK
    local_mask = lax.dynamic_slice(
        tile_mask, (row_index * blocks, col_index * col_tiles), (blocks, col_tiles)
    ).astype(jnp.float32)
    lag_basis = make_basis()
    norm_scale = 1.0 / math.sqrt(W * F)

    def fill_block(block_index, result):
        rows_here = lax.dynamic_slice_in_dim(row_block, block_index * BLK, BLK, 1)
        cross_spec = jnp.einsum(
            "fiw,fjw->fij", rows_here, both_parts, preferred_element_type=jnp.float32
        ).astype(jnp.bfloat16)
        cross_spec = cross_spec.reshape(F, BLK, 2, col_count)
        lagged = jnp.einsum(
            "lpf,fipj->lij", lag_basis, cross_spec, preferred_element_type=jnp.float32
        )
        mask_tiles = lax.dynamic_index_in_dim(local_mask, block_index, 0, keepdims=False)
        mask_row = jnp.broadcast_to(mask_tiles[:, None], (col_tiles, BLK)).reshape(col_count)
        tile_piece = (lagged * norm_scale * mask_row[None, None, :]).astype(jnp.bfloat16)
        return lax.dynamic_update_slice_in_dim(result, tile_piece, block_index * BLK, 1)

    initial = jnp.zeros((LAGS, row_count, col_count), jnp.bfloat16)
    return lax.fori_loop(0, blocks, fill_block, initial)


def solution(mesh):
    placed = (P(None, ("row", "col"), None), P(("row", "col")), P())
    return jax.shard_map(
        per_device, mesh=mesh, in_specs=placed, out_specs=P(None, "row", "col"), check_vma=False
    )
```

profile of v0, /device:TPU:7, one launch (start us, length us, event | category | flops | bytes accessed | tf_op | source)
XLA Modules:
  0.0 1225.6 jit_solution(15396092623245005193)
XLA Ops:
  15.3 288.3 %all-gather.3.cloned.1.call-done = bf16[32,512,512]{2,1,0:T(8,128)(2,1)} async-done(((bf16[32,128,512]{2,1,0:T(8,128)(2,1)}), bf16[32,512,512]{2,1,0:T(8,128)(2,1)}) %all-gather.3.cloned.1.call-update) | async-done | bytes 16777232 | tf_op jit(solution)/shard_map/all_gather | solution.py:34
  303.6 19.1 %fusion.11 = (bf16[32,512,512]{2,1,0:T(8,128)(2,1)}, bf16[32,512,512]{2,1,0:T(8,128)(2,1)}) fusion(bf16[32,512,512]{2,1,0:T(8,128)(2,1)} %all-gather.3.cloned.1.call-done, pred[]{:T(512)S(6)} %eq.6, pred[]{:T(512)S(6)} %eq.7), kind=kLoop, calls=%fused_computation.17 | loop fusion | flops 41943040 | bytes 50331648 | tf_op jit(solution)/shard_map/convert.2
  322.7 23.2 %pad_maximum_fusion = bf16[32,1024,512]{2,1,0:T(8,128)(2,1)} fusion(bf16[32,512,512]{2,1,0:T(8,128)(2,1)} %get-tuple-element.130, bf16[32,512,512]{2,1,0:T(8,128)(2,1)} %get-tuple-element.129), kind=kLoop, calls=%fused_computation.19 | loop fusion | flops 67108864 | bytes 67108864 | tf_op jit(solution)/shard_map/concatenate | solution.py:41
  345.9 202.4 %reduce-scatter.2.cloned.1.call-done = bf16[32,128,512]{2,1,0:T(8,128)(2,1)} async-done(((bf16[32,1024,512]{2,1,0:T(8,128)(2,1)}), bf16[32,128,512]{2,1,0:T(8,128)(2,1)}) %reduce-scatter.2.cloned.1.call-update) | async-done | bytes 4194320 | tf_op jit(solution)/shard_map/reduce_scatter | solution.py:42
  549.3 162.4 %all-gather.5.cloned.1.call-done = bf16[32,1024,512]{2,1,0:T(8,128)(2,1)} async-done(((bf16[32,128,512]{2,1,0:T(8,128)(2,1)}), bf16[32,1024,512]{2,1,0:T(8,128)(2,1)}) %all-gather.5.cloned.1.call-update) | async-done | bytes 33554448 | tf_op jit(solution)/shard_map/all_gather | solution.py:43
  711.6 22.5 %slice_negate_fusion = (bf16[32,1024,256]{2,1,0:T(8,128)(2,1)}, bf16[32,1024,256]{2,1,0:T(8,128)(2,1)}) fusion(bf16[32,1024,512]{2,1,0:T(8,128)(2,1)} %all-gather.5.cloned.1.call-done), kind=kLoop, calls=%fused_computation.20 | loop fusion | flops 8388608 | bytes 67108864 | tf_op jit(solution)/shard_map/neg | solution.py:45
  734.2 44.3 %maximum_maximum_fusion = bf16[32,2048,512]{2,1,0:T(8,128)(2,1)} fusion(bf16[32,1024,256]{2,1,0:T(8,128)(2,1)} %get-tuple-element.128, bf16[32,1024,256]{2,1,0:T(8,128)(2,1)} %get-tuple-element.127, bf16[32,1024,512]{2,1,0:T(8,128)(2,1)} %all-gather.5.cloned.1.call-done), kind=kLoop, calls=%fused_computation.14 | loop fusion | flops 201326592 | bytes 134217728 | tf_op jit(solution)/shard_map/concatenate | solution.py:46
  778.5 21.3 %broadcast_in_dim.28.clone = bf16[64,512,1024]{2,1,0:T(8,128)(2,1)} broadcast(bf16[]{:T(256)} %constant.68.clone.1), dimensions={} | broadcast | bytes 67108864 | tf_op jit(solution)/shard_map/broadcast_in_dim | solution.py:71
  799.7 419.4 %while.13 = (s32[]{:T(128)}, bf16[64,512,1024]{2,1,0:T(8,128)(2,1)}, bf16[32,512,512]{2,1,0:T(8,128)(2,1)}, bf16[32,2048,512]{2,1,0:T(8,128)(2,1)}, bf16[64,2,32...) while((s32[]{:T(128)}, ...), condition=%wide.region_3.4_spmd, body=%wide.region_2.3_spmd.sunk | while | flops 9688842240 | bytes 188760320 | solution.py:72
  799.8 34.9 %convolution_convert_fusion.2 = bf16[32,128,2048]{2,1,0:T(8,128)(2,1)} fusion(bf16[32,2048,512]{2,1,0:T(8,128)(2,1)} %get-tuple-element.195, bf16[32,512,512]{2,1,0:T(8,128)(2,1)} %get-tuple-element.194, s32[]{:T(128)S(6)} %select_n.49), kind=kOutput, calls=%fused_computation.6.clone.2 | convolution fusion | flops 8598323200 | bytes 88080384 | tf_op jit(solution)/shard_map/while/body/eval_jaxpr/fiw,fjw->fij/dot_general | solution.py:59
  834.7 27.8 %reshape.122 = bf16[32,128,2,1024]{3,2,1,0:T(2,128)(2,1)} reshape(bf16[32,128,2048]{2,1,0:T(8,128)(2,1)} %convolution_convert_fusion.2) | data formatting | bytes 33554432 | tf_op jit(solution)/shard_map/while/body/eval_jaxpr/reshape | solution.py:62
  862.5 23.4 %fusion.29 = bf16[64,128,1024]{2,0,1:T(8,128)(2,1)} fusion(f32[1024]{0:T(1024)S(1)} %broadcast_bitcast_fusion.2, bf16[32,128,2,1024]{3,2,1,0:T(2,128)(2,1)} %reshape.122, bf16[64,2,32]{0,2,1:T(8,128)(2,1)S(1)} %get-tuple-element.196), kind=kOutput, calls=%fused_computation.2.clone.1 | convolution fusion | flops 1090519040 | bytes 33566720 | tf_op jit(solution)/shard_map/while/body/eval_jaxpr/lpf,fipj->lij/dot_general | solution.py:63
  885.9 18.7 %copy_dynamic-update-slice_fusion.2 = bf16[64,512,1024]{2,1,0:T(8,128)(2,1)} fusion(bf16[64,512,1024]{2,1,0:T(8,128)(2,1)} %get-tuple-element.183, s32[]{:T(128)S(6)} %select_n.49, bf16[64,128,1024]{2,0,1:T(8,128)(2,1)} %fusion.29), kind=kLoop, calls=%fused_computation.3.clone.1 | loop fusion | bytes 33554436 | tf_op jit(solution)/shard_map/while/body/eval_jaxpr/dynamic_update_slice | solution.py:69
  904.7 34.9 %convolution_convert_fusion.2 = bf16[32,128,2048]{2,1,0:T(8,128)(2,1)} fusion(bf16[32,2048,512]{2,1,0:T(8,128)(2,1)} %get-tuple-element.195, bf16[32,512,512]{2,1,0:T(8,128)(2,1)} %get-tuple-element.194, s32[]{:T(128)S(6)} %select_n.49), kind=kOutput, calls=%fused_computation.6.clone.2 | convolution fusion | flops 8598323200 | bytes 88080384 | tf_op jit(solution)/shard_map/while/body/eval_jaxpr/fiw,fjw->fij/dot_general | solution.py:59
  939.5 27.8 %reshape.122 = bf16[32,128,2,1024]{3,2,1,0:T(2,128)(2,1)} reshape(bf16[32,128,2048]{2,1,0:T(8,128)(2,1)} %convolution_convert_fusion.2) | data formatting | bytes 33554432 | tf_op jit(solution)/shard_map/while/body/eval_jaxpr/reshape | solution.py:62
  967.3 23.4 %fusion.29 = bf16[64,128,1024]{2,0,1:T(8,128)(2,1)} fusion(f32[1024]{0:T(1024)S(1)} %broadcast_bitcast_fusion.2, bf16[32,128,2,1024]{3,2,1,0:T(2,128)(2,1)} %reshape.122, bf16[64,2,32]{0,2,1:T(8,128)(2,1)S(1)} %get-tuple-element.196), kind=kOutput, calls=%fused_computation.2.clone.1 | convolution fusion | flops 1090519040 | bytes 33566720 | tf_op jit(solution)/shard_map/while/body/eval_jaxpr/lpf,fipj->lij/dot_general | solution.py:63
  1009.5 34.9 %convolution_convert_fusion.2 = bf16[32,128,2048]{2,1,0:T(8,128)(2,1)} fusion(bf16[32,2048,512]{2,1,0:T(8,128)(2,1)} %get-tuple-element.195, bf16[32,512,512]{2,1,0:T(8,128)(2,1)} %get-tuple-element.194, s32[]{:T(128)S(6)} %select_n.49), kind=kOutput, calls=%fused_computation.6.clone.2 | convolution fusion | flops 8598323200 | bytes 88080384 | tf_op jit(solution)/shard_map/while/body/eval_jaxpr/fiw,fjw->fij/dot_general | solution.py:59
  1044.4 27.8 %reshape.122 = bf16[32,128,2,1024]{3,2,1,0:T(2,128)(2,1)} reshape(bf16[32,128,2048]{2,1,0:T(8,128)(2,1)} %convolution_convert_fusion.2) | data formatting | bytes 33554432 | tf_op jit(solution)/shard_map/while/body/eval_jaxpr/reshape | solution.py:62
  1072.2 23.4 %fusion.29 = bf16[64,128,1024]{2,0,1:T(8,128)(2,1)} fusion(f32[1024]{0:T(1024)S(1)} %broadcast_bitcast_fusion.2, bf16[32,128,2,1024]{3,2,1,0:T(2,128)(2,1)} %reshape.122, bf16[64,2,32]{0,2,1:T(8,128)(2,1)S(1)} %get-tuple-element.196), kind=kOutput, calls=%fused_computation.2.clone.1 | convolution fusion | flops 1090519040 | bytes 33566720 | tf_op jit(solution)/shard_map/while/body/eval_jaxpr/lpf,fipj->lij/dot_general | solution.py:63
  1095.6 18.7 %copy_dynamic-update-slice_fusion.2 = bf16[64,512,1024]{2,1,0:T(8,128)(2,1)} fusion(bf16[64,512,1024]{2,1,0:T(8,128)(2,1)} %get-tuple-element.183, s32[]{:T(128)S(6)} %select_n.49, bf16[64,128,1024]{2,0,1:T(8,128)(2,1)} %fusion.29), kind=kLoop, calls=%fused_computation.3.clone.1 | loop fusion | bytes 33554436 | tf_op jit(solution)/shard_map/while/body/eval_jaxpr/dynamic_update_slice | solution.py:69
  1114.3 34.9 %convolution_convert_fusion.2 = bf16[32,128,2048]{2,1,0:T(8,128)(2,1)} fusion(bf16[32,2048,512]{2,1,0:T(8,128)(2,1)} %get-tuple-element.195, bf16[32,512,512]{2,1,0:T(8,128)(2,1)} %get-tuple-element.194, s32[]{:T(128)S(6)} %select_n.49), kind=kOutput, calls=%fused_computation.6.clone.2 | convolution fusion | flops 8598323200 | bytes 88080384 | tf_op jit(solution)/shard_map/while/body/eval_jaxpr/fiw,fjw->fij/dot_general | solution.py:59
  1149.2 27.8 %reshape.122 = bf16[32,128,2,1024]{3,2,1,0:T(2,128)(2,1)} reshape(bf16[32,128,2048]{2,1,0:T(8,128)(2,1)} %convolution_convert_fusion.2) | data formatting | bytes 33554432 | tf_op jit(solution)/shard_map/while/body/eval_jaxpr/reshape | solution.py:62
  1177.0 23.4 %fusion.29 = bf16[64,128,1024]{2,0,1:T(8,128)(2,1)} fusion(f32[1024]{0:T(1024)S(1)} %broadcast_bitcast_fusion.2, bf16[32,128,2,1024]{3,2,1,0:T(2,128)(2,1)} %reshape.122, bf16[64,2,32]{0,2,1:T(8,128)(2,1)S(1)} %get-tuple-element.196), kind=kOutput, calls=%fused_computation.2.clone.1 | convolution fusion | flops 1090519040 | bytes 33566720 | tf_op jit(solution)/shard_map/while/body/eval_jaxpr/lpf,fipj->lij/dot_general | solution.py:63
  1200.4 18.7 %copy_dynamic-update-slice_fusion.2 = bf16[64,512,1024]{2,1,0:T(8,128)(2,1)} fusion(bf16[64,512,1024]{2,1,0:T(8,128)(2,1)} %get-tuple-element.183, s32[]{:T(128)S(6)} %select_n.49, bf16[64,128,1024]{2,0,1:T(8,128)(2,1)} %fusion.29), kind=kLoop, calls=%fused_computation.3.clone.1 | loop fusion | bytes 33554436 | tf_op jit(solution)/shard_map/while/body/eval_jaxpr/dynamic_update_slice | solution.py:69
  (26 shorter events, 28.7 us)
Async XLA Ops:
  6.5 297.0 %all-gather.3.cloned.1.call-start = ((), (), s32[]{:S(2)}) async-start(), calls=%async_computation.1 | async-start | bytes 20971520 | tf_op jit(solution)/shard_map/all_gather | solution.py:34
  15.2 533.1 %reduce-scatter.2.cloned.1.call-start = ((), (), s32[]{:S(2)}) async-start(), calls=%async_computation.2 | async-start | bytes 37748736 | tf_op jit(solution)/shard_map/reduce_scatter | solution.py:42
  345.9 365.7 %all-gather.5.cloned.1.call-start = ((), (), s32[]{:S(2)}) async-start(), calls=%async_computation.3 | async-start | bytes 37748736 | tf_op jit(solution)/shard_map/all_gather | solution.py:43
Sparse Core Ops, SparseCore 0:
  15.3 288.1 all-gather.2
  346.0 202.2 reduce-scatter.1
  550.4 161.2 all-gather.4
where the time goes:
time: 1230 us
  waiting for transfers between devices  653 us (53%)
  matrix products  233 us (19%)
  local copies, waits for them, and re-layouts  207 us (17%)
  other arithmetic  119 us (10%)
  between operations  13.2 us (1%)
    all_gather x1, waiting for transfers between devices, per_device(): row_block = lax.all_gather(white, 'col', axis=1, tiled=True)  288 us
    reduce_scatter x1, waiting for transfers between devices, per_device(): lax.psum_scatter(sectioned.astype(jnp.bfloat16), 'row', scatter_dimension...  202 us
    all_gather x1, waiting for transfers between devices, per_device(): col_block = lax.all_gather(share, 'row', axis=1, tiled=True)  162 us
    dot_general x4, matrix products, fill_block(): jnp.einsum('fiw,fjw->fij', rows_here, both_parts, preferred_element_type=...  140 us
    reshape x4, local copies, waits for them, and re-layouts, fill_block(): cross_spec = cross_spec.reshape(F, BLK, 2, col_count)  111 us
    dot_general x4, matrix products, fill_block(): jnp.einsum('lpf,fipj->lij', lag_basis, cross_spec, preferred_element_type...  93.7 us
    dynamic_update_slice x4, local copies, waits for them, and re-layouts, fill_block(): lax.dynamic_update_slice_in_dim(result, tile_piece, block_index * BLK, 1)  74.6 us
    concatenate x1, other arithmetic, per_device(): both_parts = jnp.concatenate([col_block, turned], axis=1)  44.3 us
  transfers between devices with their start and end apart: 3, of which 3 were waited for; matrix products, arithmetic and copies ran while one was open for 0% of the time, Pallas kernels for 0%

commit v1 on v0

v1 whole, which is shorter than its diff:
```python
import functools
import math

import jax
import jax.numpy as jnp
import numpy as np
from jax import lax
from jax.experimental import pallas as pl
from jax.experimental.pallas import tpu as pltpu
from jax.sharding import PartitionSpec as P

BLK = 128
LAGS = 64
PARTS = 4
GROUP = 8
VMEM_BYTES = 48 * 1024 * 1024
AXES = ("row", "col")


def whiten(spectra, quality):
    values = spectra.astype(jnp.float32)
    half_width = values.shape[2] // 2
    real_part = values[:, :, :half_width]
    imag_part = values[:, :, half_width:]
    energy = real_part * real_part + imag_part * imag_part
    mean_energy = jnp.mean(energy, axis=0, keepdims=True)
    factor = quality.astype(jnp.float32)[None, :, None] / jnp.sqrt(energy + mean_energy + 1e-06)
    return jnp.concatenate([real_part * factor, imag_part * factor], axis=2).astype(jnp.bfloat16)


def lag_angles(bins):
    lag_offset = np.arange(LAGS, dtype=np.float32) - np.float32(LAGS / 2)
    frequency = np.arange(bins, dtype=np.float32) + np.float32(1.0)
    scaled = np.float32(2.0 * math.pi) * frequency[None, :]
    return (scaled * lag_offset[:, None]) / np.float32(2.0 * LAGS)


def general_plan(mesh, spectra, quality, tile_mask):
    bins, _, width = spectra.shape
    row_size, col_size = mesh.shape["row"], mesh.shape["col"]
    white = whiten(spectra, quality)
    row_block = lax.all_gather(white, "col", axis=1, tiled=True)
    row_index, col_index = lax.axis_index("row"), lax.axis_index("col")
    row_count = row_block.shape[1]
    col_count = row_count * row_size // col_size
    share_of = row_size // col_size
    zeros = jnp.zeros_like(row_block)
    sectioned = jnp.concatenate(
        [jnp.where(row_index == share_of * col_index + s, row_block, zeros) for s in range(share_of)], axis=1
    )
    share = lax.psum_scatter(sectioned, "row", scatter_dimension=1, tiled=True)
    col_block = lax.all_gather(share, "row", axis=1, tiled=True)
    half_width = width // 2
    turned = jnp.concatenate([-col_block[:, :, half_width:], col_block[:, :, :half_width]], axis=2)
    both_parts = jnp.concatenate([col_block, turned], axis=1)
    angles = lag_angles(bins)
    basis = jnp.asarray(np.stack([np.cos(angles), -np.sin(angles)], axis=1)).astype(jnp.bfloat16)
    mask = jnp.repeat(jnp.repeat(tile_mask.astype(jnp.float32), BLK, axis=0), BLK, axis=1)
    local_mask = lax.dynamic_slice(mask, (row_index * row_count, col_index * col_count), (row_count, col_count))
    norm_scale = 1.0 / math.sqrt(half_width * bins)
    step = math.gcd(row_count, BLK)

    def fill(index, result):
        rows_here = lax.dynamic_slice_in_dim(row_block, index * step, step, 1)
        cross = jnp.einsum("fiw,fjw->fij", rows_here, both_parts, preferred_element_type=jnp.float32)
        cross = cross.astype(jnp.bfloat16).reshape(bins, step, 2, col_count)
        lagged = jnp.einsum("lpf,fipj->lij", basis, cross, preferred_element_type=jnp.float32)
        mask_rows = lax.dynamic_slice_in_dim(local_mask, index * step, step, 0)
        piece = (lagged * norm_scale * mask_rows[None]).astype(jnp.bfloat16)
        return lax.dynamic_update_slice_in_dim(result, piece, index * step, 1)

    initial = jnp.zeros((LAGS, row_count, col_count), jnp.bfloat16)
    return lax.fori_loop(0, row_count // step, fill, initial)


def whiten_kernel(spectra_ref, quality_ref, *out_refs):
    bins, _, width = spectra_ref.shape
    half_width = width // 2
    per = bins // len(out_refs)
    total = jnp.zeros((spectra_ref.shape[1], half_width), jnp.float32)
    for f in range(bins):
        real_part = spectra_ref[f, :, :half_width].astype(jnp.float32)
        imag_part = spectra_ref[f, :, half_width:].astype(jnp.float32)
        total = total + (real_part * real_part + imag_part * imag_part)
    offset = total * (1.0 / bins) + 1e-06
    quality = quality_ref[...].astype(jnp.float32)
    for f in range(bins):
        real_part = spectra_ref[f, :, :half_width].astype(jnp.float32)
        imag_part = spectra_ref[f, :, half_width:].astype(jnp.float32)
        factor = quality * lax.rsqrt(real_part * real_part + imag_part * imag_part + offset)
        out_refs[f // per][f % per, :, :half_width] = (real_part * factor).astype(jnp.bfloat16)
        out_refs[f // per][f % per, :, half_width:] = (imag_part * factor).astype(jnp.bfloat16)


def whiten_parts(spectra, quality):
    bins, channels, width = spectra.shape
    per = bins // PARTS
    rows = 16
    return pl.pallas_call(
        whiten_kernel,
        grid=(channels // rows,),
        in_specs=[
            pl.BlockSpec((bins, rows, width), lambda i: (0, i, 0)),
            pl.BlockSpec((rows, 1), lambda i: (i, 0)),
        ],
        out_specs=[pl.BlockSpec((per, rows, width), lambda i: (0, i, 0))] * PARTS,
        out_shape=[jax.ShapeDtypeStruct((per, channels, width), jnp.bfloat16)] * PARTS,
        compiler_params=pltpu.CompilerParams(vmem_limit_bytes=VMEM_BYTES),
        name="whiten",
    )(spectra, quality[:, None])


def pick_kernel(choice_ref, *refs):
    sources, target_ref, sem = refs[:-2], refs[-2], refs[-1]
    block = target_ref.shape[0]
    first = pl.program_id(0) * block
    for index, source in enumerate(sources):

        @pl.when(choice_ref[0] == index)
        def _():
            pltpu.make_async_copy(source.at[pl.ds(first, block)], target_ref, sem).start()

    pltpu.make_async_copy(sources[0].at[pl.ds(first, block)], target_ref, sem).wait()


def pick(choice, sources):
    shape = sources[0]
    moved = 2 * math.prod(shape.shape) * 2
    block = shape.shape[0] // 2
    return pl.pallas_call(
        pick_kernel,
        grid_spec=pltpu.PrefetchScalarGridSpec(
            num_scalar_prefetch=1,
            grid=(shape.shape[0] // block,),
            in_specs=[pl.BlockSpec(memory_space=pl.ANY)] * len(sources),
            out_specs=pl.BlockSpec((block,) + shape.shape[1:], lambda i, _: (i, 0, 0)),
            scratch_shapes=[pltpu.SemaphoreType.DMA],
        ),
        out_shape=jax.ShapeDtypeStruct(shape.shape, shape.dtype),
        cost_estimate=pl.CostEstimate(flops=0, bytes_accessed=moved, transcendentals=0),
        name="pick",
    )(choice, *sources)


def correlate_kernel(units, parts, offset_ref, scale_ref, *refs):
    n_sets = 1 + max(max(u) for u in units)
    x_refs = [refs[s * parts : (s + 1) * parts] for s in range(n_sets)]
    rest = refs[n_sets * parts :]
    y_refs = [[rest[(2 * s + h) * parts : (2 * s + h + 1) * parts] for h in range(2)] for s in range(n_sets)]
    rest = rest[2 * n_sets * parts :]
    even_ref, odd_ref = rest[:2]
    out_ref, x_buf, y_buf, cross, out_buf, in_sem, out_sem = rest[-7:]
    per, rows, width = x_buf.shape[1:]
    half_width = width // 2
    groups = rows // GROUP
    cols = 2 * rows
    lags = out_buf.shape[1]
    half = lags // 2
    steps = len(units) * parts

    def copies_in(a, b, c, slot):
        return [
            pltpu.make_async_copy(x_refs[a][c], x_buf.at[slot], in_sem.at[slot, 0]),
            pltpu.make_async_copy(y_refs[b][0][c], y_buf.at[slot, :, pl.ds(0, rows)], in_sem.at[slot, 1]),
            pltpu.make_async_copy(y_refs[b][1][c], y_buf.at[slot, :, pl.ds(rows, rows)], in_sem.at[slot, 2]),
        ]

    def fetch(step):
        slot = lax.rem(step, 2)
        for s in range(steps):
            a, b = units[s // parts]

            @pl.when(step == s)
            def _():
                for copy in copies_in(a, b, s % parts, slot):
                    copy.start()

    def copies_out(unit, slot):
        row = pl.multiple_of(offset_ref[0, unit], rows)
        return [
            pltpu.make_async_copy(
                out_buf.at[slot, :, :, pl.ds(h * rows, rows)],
                out_ref.at[:, pl.ds(row, rows), pl.ds(pl.multiple_of(offset_ref[1 + h, unit], rows), rows)],
                out_sem.at[slot, h],
            )
            for h in range(2)
        ]

    fetch(0)

    @pl.loop(0, steps)
    def _(step):
        slot = lax.rem(step, 2)
        unit = step // parts
        part = lax.rem(step, parts)

        @pl.when(step + 1 < steps)
        def _():
            fetch(step + 1)

        for copy in copies_in(units[0][0], units[0][1], 0, slot):
            copy.wait()

        @pl.loop(0, per // 2)
        def _(pair):
            results = []
            for f in range(2):
                x = x_buf[slot, 2 * pair + f]
                y = y_buf[slot, 2 * pair + f]
                turned = jnp.concatenate([x[:, half_width:], -x[:, :half_width]], axis=1)
                stacked = jnp.concatenate([x, turned], axis=0)
                product = lax.dot_general(stacked, y, (((1,), (1,)), ((), ())), preferred_element_type=jnp.float32)
                results.append(product.reshape(2 * groups, GROUP, cols))
            both = jnp.concatenate(results, axis=1).astype(jnp.bfloat16)
            place = pl.multiple_of((part * (per // 2) + pair) * 2 * GROUP, 2 * GROUP)
            cross[:, pl.ds(place, 2 * GROUP), :] = both

        @pl.when(part == parts - 1)
        def _():
            out_slot = lax.rem(unit, 2)

            @pl.when(unit >= 2)
            def _():
                for copy in copies_out(unit - 2, out_slot):
                    copy.wait()

            scale = jnp.concatenate(
                [jnp.full((1, 1, rows), scale_ref[h, unit], jnp.float32) for h in range(2)], axis=2
            )

            @pl.loop(0, groups // 2)
            def _(two):
                evens, odds = [], []
                for g in range(2):
                    even = jnp.dot(even_ref[...], cross[2 * two + g], preferred_element_type=jnp.float32)
                    odd = jnp.dot(odd_ref[...], cross[groups + 2 * two + g], preferred_element_type=jnp.float32)
                    evens.append(even.reshape(half + 1, GROUP, cols))
                    odds.append(odd.reshape(half, GROUP, cols))
                even = jnp.concatenate(evens, axis=1) * scale
                odd = jnp.concatenate(odds, axis=1) * scale
                here = pl.ds(pl.multiple_of(two * 2 * GROUP, 2 * GROUP), 2 * GROUP)
                out_buf[out_slot, half, here, :] = even[0].astype(jnp.bfloat16)
                out_buf[out_slot, 0, here, :] = (even[half] + odd[0]).astype(jnp.bfloat16)
                for d in range(1, half):
                    out_buf[out_slot, half + d, here, :] = (even[d] - odd[d]).astype(jnp.bfloat16)
                    out_buf[out_slot, half - d, here, :] = (even[d] + odd[d]).astype(jnp.bfloat16)

            for copy in copies_out(unit, out_slot):
                copy.start()

    for unit in range(max(0, len(units) - 2), len(units)):
        for copy in copies_out(unit, unit % 2):
            copy.wait()


def lag_matrices(bins):
    half = LAGS // 2
    angles = lag_angles(bins)[half:]
    last = -lag_angles(bins)[0]
    cosine = np.concatenate([np.cos(angles), np.cos(last)[None]], axis=0)
    sine = np.concatenate([np.sin(last)[None], np.sin(angles)[1:]], axis=0)

    def spread(table):
        table = table.astype(jnp.bfloat16).astype(np.float32)
        return jnp.asarray(np.kron(table, np.eye(GROUP, dtype=np.float32)).astype(jnp.bfloat16))

    return spread(cosine), spread(sine)


def correlate(units, offsets, scales, rows_sets, cols_sets, matrices, out, out_shape):
    parts = len(rows_sets[0])
    per, rows, width = rows_sets[0][0].shape
    bins = per * parts
    n_sets = 1 + max(max(u) for u in units)
    operands = []
    for s in range(n_sets):
        operands += rows_sets[s]
    for s in range(n_sets):
        for h in range(2):
            operands += cols_sets[s][h]
    any_spec = pl.BlockSpec(memory_space=pl.ANY)
    vmem_spec = pl.BlockSpec(memory_space=pltpu.VMEM)
    n_ops = len(operands)
    before = [] if out is None else [out]
    pairs = len(units) * rows * 2 * rows
    flops = pairs * (bins * width * 4 + 2 * LAGS * bins * GROUP)
    moved = len(units) * (3 * bins * rows * width * 2 + LAGS * 2 * rows * rows * 2)
    return pl.pallas_call(
        functools.partial(correlate_kernel, units, parts),
        grid_spec=pltpu.PrefetchScalarGridSpec(
            num_scalar_prefetch=2,
            grid=(1,),
            in_specs=[any_spec] * n_ops + [vmem_spec] * 2 + [any_spec] * len(before),
            out_specs=any_spec,
            scratch_shapes=[
                pltpu.VMEM((2, per, rows, width), jnp.bfloat16),
                pltpu.VMEM((2, per, 2 * rows, width), jnp.bfloat16),
                pltpu.VMEM((2 * rows // GROUP, bins * GROUP, 2 * rows), jnp.bfloat16),
                pltpu.VMEM((2, LAGS, rows, 2 * rows), jnp.bfloat16),
                pltpu.SemaphoreType.DMA((2, 3)),
                pltpu.SemaphoreType.DMA((2, 2)),
            ],
        ),
        out_shape=jax.ShapeDtypeStruct(out_shape, jnp.bfloat16),
        input_output_aliases={2 + n_ops + 2: 0} if before else {},
        cost_estimate=pl.CostEstimate(flops=flops, bytes_accessed=moved, transcendentals=0),
        compiler_params=pltpu.CompilerParams(vmem_limit_bytes=VMEM_BYTES),
        name="correlate",
    )(offsets, scales, *operands, *matrices, *before)


def line_sets(size):
    table = []
    for j in range(1, size):
        entry = []
        for z in range(size):
            if 2 * z < size:
                entry.append(("dn", j - 1) if z + j < size else ("up", j - size + z))
            else:
                entry.append(("up", j - 1) if z - j >= 0 else ("dn", j - 1 - z))
        table.append(entry)
    return table


def owner(z, arrival):
    way, hops = arrival
    return z + 1 + hops if way == "dn" else z - 1 - hops


def line_plan(mesh, spectra, quality, tile_mask):
    row_size, col_size = mesh.shape["row"], mesh.shape["col"]
    chips = row_size // 2
    bins, channels, _ = spectra.shape
    tiles = channels // BLK
    assert tiles == 1
    row_index, col_index = lax.axis_index("row"), lax.axis_index("col")
    core = row_index % 2
    ring = [i ^ (i >> 1) for i in range(chips)]
    place = [ring.index(k) for k in range(chips)]

    def send(values, moves):
        pairs = [(r * col_size + c, s * col_size + d) for (r, c), (s, d) in moves]
        return lax.ppermute(values, AXES, pairs)

    every = [(r, c) for r in range(row_size) for c in range(col_size)]

    def send_up(values, hop):
        return send(values, [((r, c), (r, c + 1)) for r, c in every if hop <= c < col_size - 1])

    def send_down(values, hop):
        return send(values, [((r, c), (r, c - 1)) for r, c in every if 0 < c < col_size - hop])

    def send_round(values, hop):
        moves = []
        for c in range(col_size):
            start = place[c * chips // col_size]
            for a, way in ((0, 1), (1, -1)):
                here = ring[(start + way * (hop - 1)) % chips]
                there = ring[(start + way * hop) % chips]
                moves.append(((2 * here + a, c), (2 * there + a, c)))
        return send(values, moves)

    def swap_cores(values):
        return send(values, [((r, c), (r ^ 1, c)) for r, c in every])

    distance = np.zeros((row_size, col_size), np.int32)
    for r, c in every:
        gap = place[r // 2] - place[c * chips // col_size]
        distance[r, c] = (gap if r % 2 == 0 else -gap) % chips
    my_distance = jnp.asarray(distance)[row_index, col_index].reshape(1)

    sets = line_sets(col_size)
    owners = np.array(
        [[z] + [owner(z, sets[j][z]) for j in range(col_size - 1)] for z in range(col_size)], np.int32
    )
    my_owners = jnp.asarray(owners)[col_index]

    parts = whiten_parts(spectra, quality)
    arrivals = {("dn", h): [] for h in range(col_size - 1)} | {("up", h): [] for h in range(col_size - 1)}
    for p in range(PARTS):
        down, up = parts[p], parts[p]
        for hop in range(col_size - 1):
            down, up = send_down(down, hop), send_up(up, hop)
            arrivals[("dn", hop)].append(down)
            arrivals[("up", hop)].append(up)

    rows_sets, cols_sets = [], []
    for j in range(col_size):
        if j == 0:
            mine = list(parts)
        else:
            kinds = sorted(set(sets[j - 1]))
            choice = jnp.asarray(np.array([kinds.index(k) for k in sets[j - 1]], np.int32))[col_index].reshape(1)
            mine = [pick(choice, [arrivals[k][p] for k in kinds]) for p in range(PARTS)]
        near, far = [], []
        for p in range(PARTS):
            held = [mine[p]]
            for hop in range(1, chips):
                held.append(send_round(held[-1], hop))
            near.append(pick(my_distance, held))
            far.append(swap_cores(near[-1]))
        rows_sets.append(mine)
        cols_sets.append([near, far])

    row_count = channels * col_size
    col_count = row_count * row_size // col_size
    half_cols = col_count // 2
    norm_scale = 1.0 / math.sqrt(spectra.shape[2] // 2 * bins)
    local_mask = lax.dynamic_slice(
        tile_mask,
        (row_index * (row_count // BLK), col_index * (col_count // BLK)),
        (row_count // BLK, col_count // BLK),
    ).astype(jnp.float32)
    matrices = lag_matrices(bins)
    out_shape = (LAGS, row_count, col_count)
    out = None
    for t in range(col_size):
        units = tuple((t, b) for b in range(t + 1)) + tuple((a, t) for a in range(t))
        row_owner = my_owners[np.array([a for a, _ in units])]
        col_owner = my_owners[np.array([b for _, b in units])]
        near_at = core * half_cols + col_owner * channels
        far_at = (1 - core) * half_cols + col_owner * channels
        offsets = jnp.stack([row_owner * channels, near_at, far_at]).astype(jnp.int32)
        scales = jnp.stack(
            [local_mask[row_owner, near_at // BLK], local_mask[row_owner, far_at // BLK]]
        ) * norm_scale
        out = correlate(units, offsets, scales, rows_sets, cols_sets, matrices, out, out_shape)
    return out


def solution(mesh):
    def per_device(spectra, quality, tile_mask):
        even = mesh.shape["row"] == 2 * mesh.shape["col"]
        plan = line_plan if even and spectra.shape[1] == BLK else general_plan
        return plan(mesh, spectra, quality, tile_mask)

    placed = (P(None, AXES, None), P(AXES), P())
    return jax.shard_map(
        per_device, mesh=mesh, in_specs=placed, out_specs=P(None, "row", "col"), check_vma=False
    )
```

time: 1230 us -> 648 us (0.53)
  waiting for transfers between devices: 653 us -> 133 us
  Pallas kernels: 0 us -> 287 us
  matrix products: 233 us -> 0 us
  starting transfers between devices: 0.09 us -> 201 us
  local copies, waits for them, and re-layouts: 207 us -> 18.9 us
  other arithmetic: 119 us -> 2.33 us
    all_gather x2 -> x0, waiting for transfers between devices: 451 us -> none  [the longest x1 288 us: per_device(): row_block = lax.all_gather(white, 'col', axis=1, tiled=True)]
    pallas_call x0 -> x33, Pallas kernels: none -> 287 us  [the longest x4 177 us: correlate(): pl.pallas_call(functools.partial(correlate_kernel, units, parts), grid_sp...]
    dot_general x8 -> x0, matrix products: 233 us -> none  [the longest x4 140 us: fill_block(): jnp.einsum('fiw,fjw->fij', rows_here, both_parts, preferred_element_type=...]
    reduce_scatter x1 -> x0, waiting for transfers between devices: 202 us -> none  [per_device(): lax.psum_scatter(sectioned.astype(jnp.bfloat16), 'row', scatter_dimension...]
    ppermute x0 -> x88, starting transfers between devices: none -> 201 us  [send(): return lax.ppermute(values, AXES, pairs)]
    ppermute x0 -> x88, waiting for transfers between devices: none -> 133 us  [send(): return lax.ppermute(values, AXES, pairs)]
    reshape x4 -> x0, local copies, waits for them, and re-layouts: 111 us -> none  [fill_block(): cross_spec = cross_spec.reshape(F, BLK, 2, col_count)]
    dynamic_update_slice x4 -> x0, local copies, waits for them, and re-layouts: 74.6 us -> none  [fill_block(): lax.dynamic_update_slice_in_dim(result, tile_piece, block_index * BLK, 1)]
  transfers between devices with their start and end apart: 3 -> 88, of which waited for: 3 -> 17; matrix products, arithmetic and copies ran while one was open for 0% -> 2% of each run, Pallas kernels for 0% -> 32%
where the time goes in v1:
time: 648 us; the launch traced here: 644 us
  Pallas kernels  287 us (44%)
  starting transfers between devices  201 us (31%)
  waiting for transfers between devices  133 us (21%)
  local copies, waits for them, and re-layouts  18.9 us (3%)
    ppermute x88, starting transfers between devices, send(): return lax.ppermute(values, AXES, pairs)  201 us
    pallas_call x4, Pallas kernels, correlate(): pl.pallas_call(functools.partial(correlate_kernel, units, parts), grid_sp...  177 us
    ppermute x88, waiting for transfers between devices, send(): return lax.ppermute(values, AXES, pairs)  133 us
    pallas_call x28, Pallas kernels, pick(): pl.pallas_call(pick_kernel, grid_spec=pltpu.PrefetchScalarGridSpec(num_sc...  104 us
  transfers between devices with their start and end apart: 88, of which 17 were waited for; matrix products, arithmetic and copies ran while one was open for 2% of the time, Pallas kernels for 32%

profile of v1, /device:TPU:7, one launch (start us, length us, event | category | flops | bytes accessed | tf_op | source)
XLA Modules:
  0.0 644.0 jit_solution(12011244125695003914)
XLA Ops:
  0.9 7.0 %whiten.1 = (bf16[8,128,512]{2,1,0:T(8,128)(2,1)S(1)}, bf16[8,128,512]{2,1,0:T(8,128)(2,1)S(1)}, bf16[8,128,512]{2,1,0:T(8,128)(2,1)S(1)}, bf16[8,128,512]{2,1,0:T(8,128)(2,1)}) custom-call(bf16[32,128,512]{2,1,0:T(8,128)(2,1)} %spectra_ref.1, s32[128,1]{1,0:T(8,128)S(1)} %copy.32.quality_ref), custom_call_target="tpu_custom_call" | custom-call | tf_op jit(solution)/shard_map/whiten/pallas_call | solution.py:99
  22.4 13.3 %collective-permute-done.1.refs_1_.refs_2_ = bf16[8,128,512]{2,1,0:T(8,128)(2,1)} collective-permute-done((bf16[8,128,512]{2,1,0:T(8,128)(2,1)S(1)}, bf16[8,128,512]{2,1,0:T(8,128)(2,1)}, u32[]{:S(2)}, u32[]{:S(2)}) %collective-permute-start.1) | collective-permute-done | bytes 1048608 | tf_op jit(solution)/shard_map/ppermute | solution.py:343
  44.3 13.8 %collective-permute-done.3.refs_1_.refs_2_ = bf16[8,128,512]{2,1,0:T(8,128)(2,1)S(1)} collective-permute-done((bf16[8,128,512]{2,1,0:T(8,128)(2,1)S(1)}, bf16[8,128,512]{2,1,0:T(8,128)(2,1)S(1)}, u32[]{:S(2)}, u32[]{:S(2)}) %collective-permute-start.3) | collective-permute-done | bytes 1048608 | tf_op jit(solution)/shard_map/ppermute | solution.py:343
  67.6 13.0 %collective-permute-done.5.refs_1_.refs_2_ = bf16[8,128,512]{2,1,0:T(8,128)(2,1)S(1)} collective-permute-done((bf16[8,128,512]{2,1,0:T(8,128)(2,1)S(1)}, bf16[8,128,512]{2,1,0:T(8,128)(2,1)S(1)}, u32[]{:S(2)}, u32[]{:S(2)}) %collective-permute-start.5) | collective-permute-done | bytes 1048608 | tf_op jit(solution)/shard_map/ppermute | solution.py:343
  117.5 12.5 %collective-permute-done.8.refs_0_ = bf16[8,128,512]{2,1,0:T(8,128)(2,1)} collective-permute-done((bf16[8,128,512]{2,1,0:T(8,128)(2,1)}, bf16[8,128,512]{2,1,0:T(8,128)(2,1)}, u32[]{:S(2)}, u32[]{:S(2)}) %collective-permute-start.8) | collective-permute-done | bytes 1048608 | tf_op jit(solution)/shard_map/ppermute | solution.py:343
  139.8 12.3 %collective-permute-done.10.refs_0_ = bf16[8,128,512]{2,1,0:T(8,128)(2,1)} collective-permute-done((bf16[8,128,512]{2,1,0:T(8,128)(2,1)}, bf16[8,128,512]{2,1,0:T(8,128)(2,1)}, u32[]{:S(2)}, u32[]{:S(2)}) %collective-permute-start.10) | collective-permute-done | bytes 1048608 | tf_op jit(solution)/shard_map/ppermute | solution.py:343
  157.9 17.0 %collective-permute-done.12.refs_0_ = bf16[8,128,512]{2,1,0:T(8,128)(2,1)} collective-permute-done((bf16[8,128,512]{2,1,0:T(8,128)(2,1)}, bf16[8,128,512]{2,1,0:T(8,128)(2,1)}, u32[]{:S(2)}, u32[]{:S(2)}) %collective-permute-start.12) | collective-permute-done | bytes 1048608 | tf_op jit(solution)/shard_map/ppermute | solution.py:343
  175.0 6.8 %collective-permute-start.26 = (bf16[8,128,512]{2,1,0:T(8,128)(2,1)}, bf16[8,128,512]{2,1,0:T(8,128)(2,1)}, u32[]{:S(2)}, u32[]{:S(2)}) collective-permute-start(bf16[8,128,512]{2,1,0:T(8,128)(2,1)} %collective-permute-done.25.refs_2_), channel_id=1, source_target_pairs={{24,16},{28,12},{17,1},{21,29},{10,26},{14,6},{3,11},{7,23}} | collective-permute-start | bytes 3145736 | tf_op jit(solution)/shard_map/ppermute | solution.py:343
  190.1 7.3 %collective-permute-done.14.refs_0_ = bf16[8,128,512]{2,1,0:T(8,128)(2,1)} collective-permute-done((bf16[8,128,512]{2,1,0:T(8,128)(2,1)}, bf16[8,128,512]{2,1,0:T(8,128)(2,1)}, u32[]{:S(2)}, u32[]{:S(2)}) %collective-permute-start.14) | collective-permute-done | bytes 1048608 | tf_op jit(solution)/shard_map/ppermute | solution.py:343
  198.7 6.8 %collective-permute-start.29 = (bf16[8,128,512]{2,1,0:T(8,128)(2,1)}, bf16[8,128,512]{2,1,0:T(8,128)(2,1)}, u32[]{:S(2)}, u32[]{:S(2)}) collective-permute-start(bf16[8,128,512]{2,1,0:T(8,128)(2,1)} %collective-permute-done.28.refs_2_), channel_id=1, source_target_pairs={{24,16},{28,12},{17,1},{21,29},{10,26},{14,6},{3,11},{7,23}} | collective-permute-start | bytes 3145736 | tf_op jit(solution)/shard_map/ppermute | solution.py:343
  213.9 7.0 %collective-permute-done.16.refs_1_ = bf16[8,128,512]{2,1,0:T(8,128)(2,1)} collective-permute-done((bf16[8,128,512]{2,1,0:T(8,128)(2,1)}, bf16[8,128,512]{2,1,0:T(8,128)(2,1)}, u32[]{:S(2)}, u32[]{:S(2)}) %collective-permute-start.16) | collective-permute-done | bytes 1048608 | tf_op jit(solution)/shard_map/ppermute | solution.py:343
  222.2 7.4 %collective-permute-start.32 = (bf16[8,128,512]{2,1,0:T(8,128)(2,1)}, bf16[8,128,512]{2,1,0:T(8,128)(2,1)}, u32[]{:S(2)}, u32[]{:S(2)}) collective-permute-start(bf16[8,128,512]{2,1,0:T(8,128)(2,1)} %collective-permute-done.31.refs_2_), channel_id=1, source_target_pairs={{24,16},{28,12},{17,1},{21,29},{10,26},{14,6},{3,11},{7,23}} | collective-permute-start | bytes 3145736 | tf_op jit(solution)/shard_map/ppermute | solution.py:343
  244.3 7.8 %collective-permute-start.35 = (bf16[8,128,512]{2,1,0:T(8,128)(2,1)}, bf16[8,128,512]{2,1,0:T(8,128)(2,1)}, u32[]{:S(2)}, u32[]{:S(2)}) collective-permute-start(bf16[8,128,512]{2,1,0:T(8,128)(2,1)} %collective-permute-done.34.refs_2_), channel_id=1, source_target_pairs={{24,16},{28,12},{17,1},{21,29},{10,26},{14,6},{3,11},{7,23}} | collective-permute-start | bytes 3145736 | tf_op jit(solution)/shard_map/ppermute | solution.py:343
  267.0 9.9 %collective-permute-start.36 = (bf16[8,128,512]{2,1,0:T(8,128)(2,1)}, bf16[8,128,512]{2,1,0:T(8,128)(2,1)}, u32[]{:S(2)}, u32[]{:S(2)}) collective-permute-start(bf16[8,128,512]{2,1,0:T(8,128)(2,1)} %pick.40.refs_4_.refs_8_.refs_12_.refs_16_), channel_id=1, source_target_pairs={{0,4},{1,5},{2,6},{3,7},{4,0},{5,1},{6,2},{7,3},{8,12},{9,13},{10,... | collective-permute-start | bytes 3145736 | tf_op jit(solution)/shard_map/ppermute | solution.py:343
  285.6 5.9 collective-permute-start.42
  298.1 9.0 %collective-permute-start.45 = (bf16[8,128,512]{2,1,0:T(8,128)(2,1)}, bf16[8,128,512]{2,1,0:T(8,128)(2,1)}, u32[]{:S(2)}, u32[]{:S(2)}) collective-permute-start(bf16[8,128,512]{2,1,0:T(8,128)(2,1)} %collective-permute-done.44.refs_2_), channel_id=1, source_target_pairs={{24,16},{28,12},{17,1},{21,29},{10,26},{14,6},{3,11},{7,23}} | collective-permute-start | bytes 3145736 | tf_op jit(solution)/shard_map/ppermute | solution.py:343
  318.8 5.9 collective-permute-start.48
  356.0 5.9 collective-permute-start.58
  378.0 6.3 collective-permute-start.64
  430.2 10.1 %collective-permute-done.80.refs_3_ = bf16[8,128,512]{2,1,0:T(8,128)(2,1)} collective-permute-done((bf16[8,128,512]{2,1,0:T(8,128)(2,1)}, bf16[8,128,512]{2,1,0:T(8,128)(2,1)}, u32[]{:S(2)}, u32[]{:S(2)}) %collective-permute-start.80) | collective-permute-done | bytes 1048608 | tf_op jit(solution)/shard_map/ppermute | solution.py:343
  446.4 12.6 %correlate.4.refs_26_ = bf16[64,512,1024]{2,1,0:T(8,128)(2,1)} custom-call(s32[3,1]{1,0:T(4,128)S(1)} %copy.33.offset_ref, f32[2,1]{1,0:T(2,128)S(1)} %maximum_multiply_fusion.3.scale_ref, bf16[8,128,512]{2,1,0:T(8,128)(2,1)S(1)} %copy-done.1, bf16[8,128,512]{2,1,0:T(8,128)(2,1)S(1)} %copy-done.3, bf16[8,128,512]{2,1,0:T(8,128)(2,1)S(1)} %copy-done.5, ...), custom_call_target="tpu_custom_call" | custom-call | flops 3221225472 | bytes 16777216 | tf_op jit(solution)/shard_map/correlate/pallas_call | solution.py:288
  459.0 33.6 %correlate.5.refs_38_ = bf16[64,512,1024]{2,1,0:T(8,128)(2,1)} custom-call(s32[3,3]{1,0:T(4,128)S(1)} %pad_add_fusion.2.offset_ref, f32[2,3]{1,0:T(2,128)S(1)} %maximum_multiply_fusion.2.scale_ref, bf16[8,128,512]{2,1,0:T(8,128)(2,1)S(1)} %copy-done.1, bf16[8,128,512]{2,1,0:T(8,128)(2,1)S(1)} %copy-done.3, ...), custom_call_target="tpu_custom_call", output_to_operand_aliasing={{}: (28, {})} | custom-call | flops 9663676416 | bytes 50331648 | tf_op jit(solution)/shard_map/correlate/pallas_call | solution.py:288
  511.0 54.7 %correlate.6.refs_50_ = bf16[64,512,1024]{2,1,0:T(8,128)(2,1)} custom-call(s32[3,5]{1,0:T(4,128)S(1)} %pad_add_fusion.1.offset_ref, f32[2,5]{1,0:T(2,128)S(1)} %maximum_multiply_fusion.1.scale_ref, bf16[8,128,512]{2,1,0:T(8,128)(2,1)S(1)} %copy-done.1, bf16[8,128,512]{2,1,0:T(8,128)(2,1)S(1)} %copy-done.3, ...), custom_call_target="tpu_custom_call", output_to_operand_aliasing={{}: (40, {})} | custom-call | flops 16106127360 | bytes 83886080 | tf_op jit(solution)/shard_map/correlate/pallas_call | solution.py:288
  568.1 75.7 %correlate.7 = bf16[64,512,1024]{2,1,0:T(8,128)(2,1)} custom-call(s32[3,7]{1,0:T(4,128)S(1)} %pad_add_fusion.offset_ref, f32[2,7]{1,0:T(2,128)S(1)} %maximum_multiply_fusion.scale_ref, bf16[8,128,512]{2,1,0:T(8,128)(2,1)S(1)} %copy-done.1, bf16[8,128,512]{2,1,0:T(8,128)(2,1)S(1)} %copy-done.3, ...), custom_call_target="tpu_custom_call", output_to_operand_aliasing={{}: (52, {})} | custom-call | flops 22548578304 | bytes 117440512 | tf_op jit(solution)/shard_map/correlate/pallas_call | solution.py:288
  (278 shorter events, 280.7 us)
Async XLA Ops:
  17.0 41.1 %collective-permute-start.3 = (bf16[8,128,512]{2,1,0:T(8,128)(2,1)S(1)}, bf16[8,128,512]{2,1,0:T(8,128)(2,1)S(1)}, u32[]{:S(2)}, u32[]{:S(2)}) collective-permute-start(bf16[8,128,512]{2,1,0:T(8,128)(2,1)S(1)} %get-tuple-element.10.refs_0_.refs_1_), channel_id=1, source_target_pairs={{0,1},{1,2},{2,3},{4,5},{5,6},{6,7},{8,9},{9,10},{10,11},{12,13},{... | collective-permute-start | bytes 3145736 | tf_op jit(solution)/shard_map/ppermute | solution.py:343
  21.1 41.8 %collective-permute-start.2 = (bf16[8,128,512]{2,1,0:T(8,128)(2,1)S(1)}, bf16[8,128,512]{2,1,0:T(8,128)(2,1)S(1)}, u32[]{:S(2)}, u32[]{:S(2)}) collective-permute-start(bf16[8,128,512]{2,1,0:T(8,128)(2,1)S(1)} %get-tuple-element.10.refs_0_.refs_1_), channel_id=1, source_target_pairs={{1,0},{2,1},{3,2},{5,4},{6,5},{7,6},{9,8},{10,9},{11,10},{13,12},{... | collective-permute-start | bytes 3145736 | tf_op jit(solution)/shard_map/ppermute | solution.py:343
  40.5 40.1 %collective-permute-start.5 = (bf16[8,128,512]{2,1,0:T(8,128)(2,1)S(1)}, bf16[8,128,512]{2,1,0:T(8,128)(2,1)S(1)}, u32[]{:S(2)}, u32[]{:S(2)}) collective-permute-start(bf16[8,128,512]{2,1,0:T(8,128)(2,1)S(1)} %get-tuple-element.11.refs_0_.refs_2_), channel_id=1, source_target_pairs={{0,1},{1,2},{2,3},{4,5},{5,6},{6,7},{8,9},{9,10},{10,11},{12,13},{... | collective-permute-start | bytes 3145736 | tf_op jit(solution)/shard_map/ppermute | solution.py:343
  43.0 42.3 %collective-permute-start.4 = (bf16[8,128,512]{2,1,0:T(8,128)(2,1)S(1)}, bf16[8,128,512]{2,1,0:T(8,128)(2,1)S(1)}, u32[]{:S(2)}, u32[]{:S(2)}) collective-permute-start(bf16[8,128,512]{2,1,0:T(8,128)(2,1)S(1)} %get-tuple-element.11.refs_0_.refs_2_), channel_id=1, source_target_pairs={{1,0},{2,1},{3,2},{5,4},{6,5},{7,6},{9,8},{10,9},{11,10},{13,12},{... | collective-permute-start | bytes 3145736 | tf_op jit(solution)/shard_map/ppermute | solution.py:343
  58.1 37.6 %collective-permute-start.33 = (bf16[8,128,512]{2,1,0:T(8,128)(2,1)}, bf16[8,128,512]{2,1,0:T(8,128)(2,1)}, u32[]{:S(2)}, u32[]{:S(2)}) collective-permute-start(bf16[8,128,512]{2,1,0:T(8,128)(2,1)} %get-tuple-element.12.refs_0_.refs_3_), channel_id=1, source_target_pairs={{0,8},{4,20},{9,25},{13,5},{18,2},{22,30},{27,19},{31,15}} | collective-permute-start | bytes 3145736 | tf_op jit(solution)/shard_map/ppermute | solution.py:343
  62.9 40.3 %collective-permute-start.7 = (bf16[8,128,512]{2,1,0:T(8,128)(2,1)}, bf16[8,128,512]{2,1,0:T(8,128)(2,1)}, u32[]{:S(2)}, u32[]{:S(2)}) collective-permute-start(bf16[8,128,512]{2,1,0:T(8,128)(2,1)} %get-tuple-element.12.refs_0_.refs_3_), channel_id=1, source_target_pairs={{0,1},{1,2},{2,3},{4,5},{5,6},{6,7},{8,9},{9,10},{10,11},{12,13},{... | collective-permute-start | bytes 3145736 | tf_op jit(solution)/shard_map/ppermute | solution.py:343
  66.3 41.6 %collective-permute-start.6 = (bf16[8,128,512]{2,1,0:T(8,128)(2,1)}, bf16[8,128,512]{2,1,0:T(8,128)(2,1)}, u32[]{:S(2)}, u32[]{:S(2)}) collective-permute-start(bf16[8,128,512]{2,1,0:T(8,128)(2,1)} %get-tuple-element.12.refs_0_.refs_3_), channel_id=1, source_target_pairs={{1,0},{2,1},{3,2},{5,4},{6,5},{7,6},{9,8},{10,9},{11,10},{13,12},{... | collective-permute-start | bytes 3145736 | tf_op jit(solution)/shard_map/ppermute | solution.py:343
  116.2 35.8 %collective-permute-start.10 = (bf16[8,128,512]{2,1,0:T(8,128)(2,1)}, bf16[8,128,512]{2,1,0:T(8,128)(2,1)}, u32[]{:S(2)}, u32[]{:S(2)}) collective-permute-start(bf16[8,128,512]{2,1,0:T(8,128)(2,1)} %copy-done.14), channel_id=1, source_target_pairs={{1,0},{2,1},{5,4},{6,5},{9,8},{10,9},{13,12},{14,13},{17,16},{18,1... | collective-permute-start | bytes 3145736 | tf_op jit(solution)/shard_map/ppermute | solution.py:343
  134.7 40.3 %collective-permute-start.12 = (bf16[8,128,512]{2,1,0:T(8,128)(2,1)}, bf16[8,128,512]{2,1,0:T(8,128)(2,1)}, u32[]{:S(2)}, u32[]{:S(2)}) collective-permute-start(bf16[8,128,512]{2,1,0:T(8,128)(2,1)} %copy-done.12), channel_id=1, source_target_pairs={{1,0},{2,1},{5,4},{6,5},{9,8},{10,9},{13,12},{14,13},{17,16},{18,1... | collective-permute-start | bytes 3145736 | tf_op jit(solution)/shard_map/ppermute | solution.py:343
  152.0 33.5 %collective-permute-start.34 = (bf16[8,128,512]{2,1,0:T(8,128)(2,1)}, bf16[8,128,512]{2,1,0:T(8,128)(2,1)}, u32[]{:S(2)}, u32[]{:S(2)}) collective-permute-start(bf16[8,128,512]{2,1,0:T(8,128)(2,1)} %collective-permute-done.33.refs_1_), channel_id=1, source_target_pairs={{8,24},{20,28},{25,17},{5,21},{2,10},{30,14},{19,3},{15,7}} | collective-permute-start | bytes 3145736 | tf_op jit(solution)/shard_map/ppermute | solution.py:343
  153.3 33.8 %collective-permute-start.15 = (bf16[8,128,512]{2,1,0:T(8,128)(2,1)}, bf16[8,128,512]{2,1,0:T(8,128)(2,1)}, u32[]{:S(2)}, u32[]{:S(2)}) collective-permute-start(bf16[8,128,512]{2,1,0:T(8,128)(2,1)} %collective-permute-done.7.refs_1_.refs_2_), channel_id=1, source_target_pairs={{1,2},{2,3},{5,6},{6,7},{9,10},{10,11},{13,14},{14,15},{17,18},{18... | collective-permute-start | bytes 3145736 | tf_op jit(solution)/shard_map/ppermute | solution.py:343
  155.0 33.4 %collective-permute-start.49 = (bf16[8,128,512]{2,1,0:T(8,128)(2,1)}, bf16[8,128,512]{2,1,0:T(8,128)(2,1)}, u32[]{:S(2)}, u32[]{:S(2)}) collective-permute-start(bf16[8,128,512]{2,1,0:T(8,128)(2,1)} %pick.31.refs_0_.refs_7_), channel_id=1, source_target_pairs={{0,8},{4,20},{9,25},{13,5},{18,2},{22,30},{27,19},{31,15}} | collective-permute-start | bytes 3145736 | tf_op jit(solution)/shard_map/ppermute | solution.py:343
  156.7 40.8 %collective-permute-start.14 = (bf16[8,128,512]{2,1,0:T(8,128)(2,1)}, bf16[8,128,512]{2,1,0:T(8,128)(2,1)}, u32[]{:S(2)}, u32[]{:S(2)}) collective-permute-start(bf16[8,128,512]{2,1,0:T(8,128)(2,1)} %collective-permute-done.6.refs_0_), channel_id=1, source_target_pairs={{1,0},{2,1},{5,4},{6,5},{9,8},{10,9},{13,12},{14,13},{17,16},{18,1... | collective-permute-start | bytes 3145736 | tf_op jit(solution)/shard_map/ppermute | solution.py:343
  267.0 31.1 %collective-permute-start.36 = (bf16[8,128,512]{2,1,0:T(8,128)(2,1)}, bf16[8,128,512]{2,1,0:T(8,128)(2,1)}, u32[]{:S(2)}, u32[]{:S(2)}) collective-permute-start(bf16[8,128,512]{2,1,0:T(8,128)(2,1)} %pick.40.refs_4_.refs_8_.refs_12_.refs_16_), channel_id=1, source_target_pairs={{0,4},{1,5},{2,6},{3,7},{4,0},{5,1},{6,2},{7,3},{8,12},{9,13},{10,... | collective-permute-start | bytes 3145736 | tf_op jit(solution)/shard_map/ppermute | solution.py:343
  407.1 33.2 %collective-permute-start.80 = (bf16[8,128,512]{2,1,0:T(8,128)(2,1)}, bf16[8,128,512]{2,1,0:T(8,128)(2,1)}, u32[]{:S(2)}, u32[]{:S(2)}) collective-permute-start(bf16[8,128,512]{2,1,0:T(8,128)(2,1)} %collective-permute-done.79.refs_2_), channel_id=1, source_target_pairs={{24,16},{28,12},{17,1},{21,29},{10,26},{14,6},{3,11},{7,23}} | collective-permute-start | bytes 3145736 | tf_op jit(solution)/shard_map/ppermute | solution.py:343
  426.4 82.7 %collective-permute-start.68 = (bf16[8,128,512]{2,1,0:T(8,128)(2,1)}, bf16[8,128,512]{2,1,0:T(8,128)(2,1)}, u32[]{:S(2)}, u32[]{:S(2)}) collective-permute-start(bf16[8,128,512]{2,1,0:T(8,128)(2,1)} %pick.48.refs_28_.refs_32_), channel_id=1, source_target_pairs={{0,4},{1,5},{2,6},{3,7},{4,0},{5,1},{6,2},{7,3},{8,12},{9,13},{10,... | collective-permute-start | bytes 3145736 | tf_op jit(solution)/shard_map/ppermute | solution.py:343
  428.2 81.0 %collective-permute-start.69 = (bf16[8,128,512]{2,1,0:T(8,128)(2,1)}, bf16[8,128,512]{2,1,0:T(8,128)(2,1)}, u32[]{:S(2)}, u32[]{:S(2)}) collective-permute-start(bf16[8,128,512]{2,1,0:T(8,128)(2,1)} %pick.49.refs_29_.refs_33_), channel_id=1, source_target_pairs={{0,4},{1,5},{2,6},{3,7},{4,0},{5,1},{6,2},{7,3},{8,12},{9,13},{10,... | collective-permute-start | bytes 3145736 | tf_op jit(solution)/shard_map/ppermute | solution.py:343
  428.3 81.4 %collective-permute-start.70 = (bf16[8,128,512]{2,1,0:T(8,128)(2,1)}, bf16[8,128,512]{2,1,0:T(8,128)(2,1)}, u32[]{:S(2)}, u32[]{:S(2)}) collective-permute-start(bf16[8,128,512]{2,1,0:T(8,128)(2,1)} %pick.50.refs_30_.refs_34_), channel_id=1, source_target_pairs={{0,4},{1,5},{2,6},{3,7},{4,0},{5,1},{6,2},{7,3},{8,12},{9,13},{10,... | collective-permute-start | bytes 3145736 | tf_op jit(solution)/shard_map/ppermute | solution.py:343
  429.1 80.7 %collective-permute-start.71 = (bf16[8,128,512]{2,1,0:T(8,128)(2,1)}, bf16[8,128,512]{2,1,0:T(8,128)(2,1)}, u32[]{:S(2)}, u32[]{:S(2)}) collective-permute-start(bf16[8,128,512]{2,1,0:T(8,128)(2,1)} %pick.51.refs_31_.refs_35_), channel_id=1, source_target_pairs={{0,4},{1,5},{2,6},{3,7},{4,0},{5,1},{6,2},{7,3},{8,12},{9,13},{10,... | collective-permute-start | bytes 3145736 | tf_op jit(solution)/shard_map/ppermute | solution.py:343
  440.3 63.4 %collective-permute-start.83 = (bf16[8,128,512]{2,1,0:T(8,128)(2,1)}, bf16[8,128,512]{2,1,0:T(8,128)(2,1)}, u32[]{:S(2)}, u32[]{:S(2)}) collective-permute-start(bf16[8,128,512]{2,1,0:T(8,128)(2,1)} %collective-permute-done.82.refs_2_), channel_id=1, source_target_pairs={{24,16},{28,12},{17,1},{21,29},{10,26},{14,6},{3,11},{7,23}} | collective-permute-start | bytes 3145736 | tf_op jit(solution)/shard_map/ppermute | solution.py:343
  503.7 62.0 %collective-permute-start.84 = (bf16[8,128,512]{2,1,0:T(8,128)(2,1)}, bf16[8,128,512]{2,1,0:T(8,128)(2,1)}, u32[]{:S(2)}, u32[]{:S(2)}) collective-permute-start(bf16[8,128,512]{2,1,0:T(8,128)(2,1)} %pick.52.refs_40_), channel_id=1, source_target_pairs={{0,4},{1,5},{2,6},{3,7},{4,0},{5,1},{6,2},{7,3},{8,12},{9,13},{10,... | collective-permute-start | bytes 3145736 | tf_op jit(solution)/shard_map/ppermute | solution.py:343
  509.1 56.6 %collective-permute-start.85 = (bf16[8,128,512]{2,1,0:T(8,128)(2,1)}, bf16[8,128,512]{2,1,0:T(8,128)(2,1)S(1)}, u32[]{:S(2)}, u32[]{:S(2)}) collective-permute-start(bf16[8,128,512]{2,1,0:T(8,128)(2,1)} %pick.53.refs_41_), channel_id=1, source_target_pairs={{0,4},{1,5},{2,6},{3,7},{4,0},{5,1},{6,2},{7,3},{8,12},{9,13},{10,... | collective-permute-start | bytes 3145736 | tf_op jit(solution)/shard_map/ppermute | solution.py:343
  509.2 56.5 %collective-permute-start.86 = (bf16[8,128,512]{2,1,0:T(8,128)(2,1)}, bf16[8,128,512]{2,1,0:T(8,128)(2,1)S(1)}, u32[]{:S(2)}, u32[]{:S(2)}) collective-permute-start(bf16[8,128,512]{2,1,0:T(8,128)(2,1)} %pick.54.refs_42_), channel_id=1, source_target_pairs={{0,4},{1,5},{2,6},{3,7},{4,0},{5,1},{6,2},{7,3},{8,12},{9,13},{10,... | collective-permute-start | bytes 3145736 | tf_op jit(solution)/shard_map/ppermute | solution.py:343
  509.7 56.1 %collective-permute-start.87 = (bf16[8,128,512]{2,1,0:T(8,128)(2,1)}, bf16[8,128,512]{2,1,0:T(8,128)(2,1)S(1)}, u32[]{:S(2)}, u32[]{:S(2)}) collective-permute-start(bf16[8,128,512]{2,1,0:T(8,128)(2,1)} %pick.55.refs_43_), channel_id=1, source_target_pairs={{0,4},{1,5},{2,6},{3,7},{4,0},{5,1},{6,2},{7,3},{8,12},{9,13},{10,... | collective-permute-start | bytes 3145736 | tf_op jit(solution)/shard_map/ppermute | solution.py:343
  (89 other events, 5936.8 us)

commit v2 on v1

v2 whole, which is shorter than its diff:
```python
import functools
import math

import jax
import jax.numpy as jnp
import numpy as np
from jax import lax
from jax.experimental import pallas as pl
from jax.experimental.pallas import tpu as pltpu
from jax.sharding import PartitionSpec as P

BLK = 128
LAGS = 64
PARTS = 4
STEP_BINS = 8
GROUP = 8
VMEM_BYTES = 58 * 1024 * 1024
AXES = ("row", "col")
DEPTH = 3
LIGHT = pl.CostEstimate(flops=0, bytes_accessed=1024, transcendentals=0)
TOKEN = jax.ShapeDtypeStruct((8, 128), jnp.int32)


def whiten(spectra, quality):
    values = spectra.astype(jnp.float32)
    half_width = values.shape[2] // 2
    real_part = values[:, :, :half_width]
    imag_part = values[:, :, half_width:]
    energy = real_part * real_part + imag_part * imag_part
    mean_energy = jnp.mean(energy, axis=0, keepdims=True)
    factor = quality.astype(jnp.float32)[None, :, None] / jnp.sqrt(energy + mean_energy + 1e-06)
    return jnp.concatenate([real_part * factor, imag_part * factor], axis=2).astype(jnp.bfloat16)


def lag_angles(bins):
    lag_offset = np.arange(LAGS, dtype=np.float32) - np.float32(LAGS / 2)
    frequency = np.arange(bins, dtype=np.float32) + np.float32(1.0)
    scaled = np.float32(2.0 * math.pi) * frequency[None, :]
    return (scaled * lag_offset[:, None]) / np.float32(2.0 * LAGS)


def general_plan(mesh, spectra, quality, tile_mask):
    bins, _, width = spectra.shape
    row_size, col_size = mesh.shape["row"], mesh.shape["col"]
    white = whiten(spectra, quality)
    row_block = lax.all_gather(white, "col", axis=1, tiled=True)
    row_index, col_index = lax.axis_index("row"), lax.axis_index("col")
    row_count = row_block.shape[1]
    col_count = row_count * row_size // col_size
    share_of = row_size // col_size
    zeros = jnp.zeros_like(row_block)
    sectioned = jnp.concatenate(
        [jnp.where(row_index == share_of * col_index + s, row_block, zeros) for s in range(share_of)], axis=1
    )
    share = lax.psum_scatter(sectioned, "row", scatter_dimension=1, tiled=True)
    col_block = lax.all_gather(share, "row", axis=1, tiled=True)
    half_width = width // 2
    turned = jnp.concatenate([-col_block[:, :, half_width:], col_block[:, :, :half_width]], axis=2)
    both_parts = jnp.concatenate([col_block, turned], axis=1)
    angles = lag_angles(bins)
    basis = jnp.asarray(np.stack([np.cos(angles), -np.sin(angles)], axis=1)).astype(jnp.bfloat16)
    mask = jnp.repeat(jnp.repeat(tile_mask.astype(jnp.float32), BLK, axis=0), BLK, axis=1)
    local_mask = lax.dynamic_slice(mask, (row_index * row_count, col_index * col_count), (row_count, col_count))
    norm_scale = 1.0 / math.sqrt(half_width * bins)
    step = math.gcd(row_count, BLK)

    def fill(index, result):
        rows_here = lax.dynamic_slice_in_dim(row_block, index * step, step, 1)
        cross = jnp.einsum("fiw,fjw->fij", rows_here, both_parts, preferred_element_type=jnp.float32)
        cross = cross.astype(jnp.bfloat16).reshape(bins, step, 2, col_count)
        lagged = jnp.einsum("lpf,fipj->lij", basis, cross, preferred_element_type=jnp.float32)
        mask_rows = lax.dynamic_slice_in_dim(local_mask, index * step, step, 0)
        piece = (lagged * norm_scale * mask_rows[None]).astype(jnp.bfloat16)
        return lax.dynamic_update_slice_in_dim(result, piece, index * step, 1)

    initial = jnp.zeros((LAGS, row_count, col_count), jnp.bfloat16)
    return lax.fori_loop(0, row_count // step, fill, initial)


def whiten_kernel(spectra_ref, quality_ref, *out_refs):
    bins, _, width = spectra_ref.shape
    half_width = width // 2
    total = jnp.zeros((spectra_ref.shape[1], half_width), jnp.float32)
    for f in range(bins):
        real_part = spectra_ref[f, :, :half_width].astype(jnp.float32)
        imag_part = spectra_ref[f, :, half_width:].astype(jnp.float32)
        total = total + (real_part * real_part + imag_part * imag_part)
    offset = total * (1.0 / bins) + 1e-06
    quality = quality_ref[...].astype(jnp.float32)
    for f in range(bins):
        real_part = spectra_ref[f, :, :half_width].astype(jnp.float32)
        imag_part = spectra_ref[f, :, half_width:].astype(jnp.float32)
        factor = quality * lax.rsqrt(real_part * real_part + imag_part * imag_part + offset)
        white_real = (real_part * factor).astype(jnp.bfloat16)
        white_imag = (imag_part * factor).astype(jnp.bfloat16)
        first = 0
        for out_ref in out_refs:
            size = out_ref.shape[0]
            if first <= f % bins < first + size:
                out_ref[f - first, :, :half_width] = white_real
                out_ref[f - first, :, half_width:] = white_imag
            first = (first + size) % bins


def whiten_parts(spectra, quality, sizes):
    bins, channels, width = spectra.shape
    rows = 16
    return pl.pallas_call(
        whiten_kernel,
        grid=(channels // rows,),
        in_specs=[
            pl.BlockSpec((bins, rows, width), lambda i: (0, i, 0)),
            pl.BlockSpec((rows, 1), lambda i: (i, 0)),
        ],
        out_specs=[pl.BlockSpec((size, rows, width), lambda i: (0, i, 0)) for size in sizes],
        out_shape=[jax.ShapeDtypeStruct((size, channels, width), jnp.bfloat16) for size in sizes],
        compiler_params=pltpu.CompilerParams(vmem_limit_bytes=VMEM_BYTES),
        name="whiten",
    )(spectra, quality[:, None])


def pick_kernel(starts, choice_ref, *refs):
    sources, (target_ref, buffer, in_sem, out_sem) = refs[: len(starts)], refs[-4:]
    pieces = in_sem.shape[0]
    block = target_ref.shape[0] // pieces

    def copy_in(index, piece):
        return pltpu.make_async_copy(
            sources[index].at[pl.ds(starts[index] + piece * block, block)],
            buffer.at[pl.ds(piece * block, block)],
            in_sem.at[piece],
        )

    def copy_out(piece):
        here = pl.ds(piece * block, block)
        return pltpu.make_async_copy(buffer.at[here], target_ref.at[here], out_sem.at[piece])

    for index in range(len(starts)):

        @pl.when(choice_ref[0] == index)
        def _():
            for piece in range(pieces):
                copy_in(index, piece).start()

    for piece in range(pieces):
        copy_in(0, piece).wait()
        copy_out(piece).start()
    for piece in range(pieces):
        copy_out(piece).wait()


def pick(choice, sources, starts, size, *after):
    shape = (size,) + sources[0].shape[1:]
    pieces = min(4, size)
    any_spec = pl.BlockSpec(memory_space=pl.ANY)
    return pl.pallas_call(
        functools.partial(pick_kernel, tuple(starts)),
        grid_spec=pltpu.PrefetchScalarGridSpec(
            num_scalar_prefetch=1,
            grid=(1,),
            in_specs=[any_spec] * (len(sources) + len(after)),
            out_specs=any_spec,
            scratch_shapes=[
                pltpu.VMEM(shape, jnp.bfloat16),
                pltpu.SemaphoreType.DMA((pieces,)),
                pltpu.SemaphoreType.DMA((pieces,)),
            ],
        ),
        out_shape=jax.ShapeDtypeStruct(shape, jnp.bfloat16),
        cost_estimate=LIGHT,
        compiler_params=pltpu.CompilerParams(vmem_limit_bytes=VMEM_BYTES),
        name="pick",
    )(choice, *sources, *after)


def hold(value, *after):
    any_spec = pl.BlockSpec(memory_space=pl.ANY)
    return pl.pallas_call(
        lambda *refs: None,
        in_specs=[any_spec] * (1 + len(after)),
        out_specs=any_spec,
        out_shape=jax.ShapeDtypeStruct(value.shape, value.dtype),
        input_output_aliases={0: 0},
        cost_estimate=LIGHT,
        compiler_params=pltpu.CompilerParams(vmem_limit_bytes=VMEM_BYTES),
        name="hold",
    )(value, *after)


def correlate_kernel(row_sets, col_sets, x_from, y_from, offset_ref, scale_ref, *refs):
    n_rows, n_cols, parts = len(x_from), len(y_from), len(x_from[0])
    rest = refs[1 + max(index for one in y_from for half in one for index, _ in half) :]
    even_ref, odd_ref = rest[:2]
    out_ref, _, x_buf, y_buf, cross, out_buf, in_sem, out_sem = rest[-8:]
    per, rows, width = x_buf.shape[1:]
    half_width = width // 2
    groups = rows // GROUP
    cols = 2 * rows
    half = out_buf.shape[1] // 2
    units = n_rows * n_cols
    steps = units * parts
    x_stays, y_stays = n_rows == 1, n_cols == 1

    def source(where):
        index, start = where
        return refs[index].at[pl.ds(start, per)]

    def x_copy(s, c, slot, step):
        return [pltpu.make_async_copy(source(x_from[s][c]), x_buf.at[slot], in_sem.at[lax.rem(step, DEPTH), 0])]

    def y_copies(s, c, slot, step):
        return [
            pltpu.make_async_copy(
                source(y_from[s][h][c]), y_buf.at[slot, :, pl.ds(h * rows, rows)], in_sem.at[lax.rem(step, DEPTH), 1 + h]
            )
            for h in range(2)
        ]

    def slot_of(stays, step):
        return lax.rem(step, parts) if stays else lax.rem(step, DEPTH)

    def fetch(step):
        for s in range(steps):
            unit, c = s // parts, s % parts

            @pl.when(step == s)
            def _():
                if unit == 0 or not x_stays:
                    for copy in x_copy(0 if x_stays else unit, c, slot_of(x_stays, step), step):
                        copy.start()
                if unit == 0 or not y_stays:
                    for copy in y_copies(0 if y_stays else unit, c, slot_of(y_stays, step), step):
                        copy.start()

    def arrive(step):
        def x_wait():
            for copy in x_copy(0, 0, 0, step):
                copy.wait()

        def y_wait():
            for copy in y_copies(0, 0, 0, step):
                copy.wait()

        if x_stays:
            pl.when(step < parts)(x_wait)
        else:
            x_wait()
        if y_stays:
            pl.when(step < parts)(y_wait)
        else:
            y_wait()

    def sets_of(unit):
        return row_sets[0] + (0 if x_stays else unit), col_sets[0] + (0 if y_stays else unit)

    def copies_out(unit, slot):
        row_set, col_set = sets_of(unit)
        row = pl.multiple_of(offset_ref[0, row_set], rows)
        return [
            pltpu.make_async_copy(
                out_buf.at[slot, :, :, pl.ds(h * rows, rows)],
                out_ref.at[:, pl.ds(row, rows), pl.ds(pl.multiple_of(offset_ref[1 + h, col_set], rows), rows)],
                out_sem.at[slot, h],
            )
            for h in range(2)
        ]

    for step in range(min(DEPTH - 1, steps)):
        fetch(jnp.int32(step))

    @pl.loop(0, steps)
    def _(step):
        unit = step // parts
        part = lax.rem(step, parts)
        x_slot, y_slot = slot_of(x_stays, step), slot_of(y_stays, step)

        @pl.when(step + (DEPTH - 1) < steps)
        def _():
            fetch(step + (DEPTH - 1))

        arrive(step)

        @pl.loop(0, per // 2, unroll=True)
        def _(pair):
            results = []
            for f in range(2):
                x = x_buf[x_slot, 2 * pair + f]
                y = y_buf[y_slot, 2 * pair + f]
                turned = jnp.concatenate([x[:, half_width:], -x[:, :half_width]], axis=1)
                stacked = jnp.concatenate([x, turned], axis=0)
                product = lax.dot_general(stacked, y, (((1,), (1,)), ((), ())), preferred_element_type=jnp.float32)
                results.append(product.reshape(2 * groups, GROUP, cols))
            both = jnp.concatenate(results, axis=1).astype(jnp.bfloat16)
            at = pl.multiple_of((part * (per // 2) + pair) * 2 * GROUP, 2 * GROUP)
            cross[:, pl.ds(at, 2 * GROUP), :] = both

        @pl.when(part == parts - 1)
        def _():
            out_slot = lax.rem(unit, 2)

            @pl.when(unit >= 2)
            def _():
                for copy in copies_out(unit - 2, out_slot):
                    copy.wait()

            row_set, col_set = sets_of(unit)
            scale = jnp.concatenate(
                [jnp.full((1, 1, rows), scale_ref[row_set, 2 * col_set + h], jnp.float32) for h in range(2)], axis=2
            )

            @pl.loop(0, groups // 2, unroll=True)
            def _(two):
                evens, odds = [], []
                for g in range(2):
                    even = jnp.dot(even_ref[...], cross[2 * two + g], preferred_element_type=jnp.float32)
                    odd = jnp.dot(odd_ref[...], cross[groups + 2 * two + g], preferred_element_type=jnp.float32)
                    evens.append(even.reshape(half + 1, GROUP, cols))
                    odds.append(odd.reshape(half, GROUP, cols))
                even = jnp.concatenate(evens, axis=1) * scale
                odd = jnp.concatenate(odds, axis=1) * scale
                here = pl.ds(pl.multiple_of(two * 2 * GROUP, 2 * GROUP), 2 * GROUP)
                out_buf[out_slot, half, here, :] = even[0].astype(jnp.bfloat16)
                out_buf[out_slot, 0, here, :] = (even[half] + odd[0]).astype(jnp.bfloat16)
                for d in range(1, half):
                    out_buf[out_slot, half + d, here, :] = (even[d] - odd[d]).astype(jnp.bfloat16)
                    out_buf[out_slot, half - d, here, :] = (even[d] + odd[d]).astype(jnp.bfloat16)

            for copy in copies_out(unit, out_slot):
                copy.start()

    for unit in range(max(0, units - 2), units):
        for copy in copies_out(unit, unit % 2):
            copy.wait()


def correlate(row_sets, col_sets, offsets, scales, rows_of, cols_of, matrices, out, out_shape, after):
    operands = []

    def spread(arrays):
        where = []
        for array in arrays:
            where += [(len(operands), start) for start in range(0, array.shape[0], STEP_BINS)]
            operands.append(array)
        return tuple(where)

    x_from = tuple(spread(rows_of[s]) for s in row_sets)
    y_from = tuple(tuple(spread(half) for half in cols_of[s]) for s in col_sets)
    parts, per = len(x_from[0]), STEP_BINS
    _, rows, width = operands[0].shape
    bins = per * parts
    before = [] if out is None else [out]
    units = len(row_sets) * len(col_sets)
    any_spec = pl.BlockSpec(memory_space=pl.ANY)
    vmem_spec = pl.BlockSpec(memory_space=pltpu.VMEM)
    n_ops = len(operands)
    x_slots = parts if len(row_sets) == 1 else DEPTH
    y_slots = parts if len(col_sets) == 1 else DEPTH
    return pl.pallas_call(
        functools.partial(correlate_kernel, row_sets, col_sets, x_from, y_from),
        grid_spec=pltpu.PrefetchScalarGridSpec(
            num_scalar_prefetch=2,
            grid=(1,),
            in_specs=[any_spec] * n_ops + [vmem_spec] * 2 + [any_spec] * (len(before) + 1),
            out_specs=[any_spec, any_spec],
            scratch_shapes=[
                pltpu.VMEM((x_slots, per, rows, width), jnp.bfloat16),
                pltpu.VMEM((y_slots, per, 2 * rows, width), jnp.bfloat16),
                pltpu.VMEM((2 * rows // GROUP, bins * GROUP, 2 * rows), jnp.bfloat16),
                pltpu.VMEM((2, LAGS, rows, 2 * rows), jnp.bfloat16),
                pltpu.SemaphoreType.DMA((DEPTH, 3)),
                pltpu.SemaphoreType.DMA((2, 2)),
            ],
        ),
        out_shape=[jax.ShapeDtypeStruct(out_shape, jnp.bfloat16), TOKEN],
        input_output_aliases={2 + n_ops + 2: 0} if before else {},
        cost_estimate=LIGHT,
        compiler_params=pltpu.CompilerParams(vmem_limit_bytes=VMEM_BYTES),
        name="correlate",
    )(offsets, scales, *operands, *matrices, *before, after)


def lag_matrices(bins):
    half = LAGS // 2
    angles = lag_angles(bins)[half:]
    last = -lag_angles(bins)[0]
    cosine = np.concatenate([np.cos(angles), np.cos(last)[None]], axis=0)
    sine = np.concatenate([np.sin(last)[None], np.sin(angles)[1:]], axis=0)

    def spread(table):
        table = table.astype(jnp.bfloat16).astype(np.float32)
        return jnp.asarray(np.kron(table, np.eye(GROUP, dtype=np.float32)).astype(jnp.bfloat16))

    return spread(cosine), spread(sine)


def line_plan(mesh, spectra, quality, tile_mask):
    row_size, col_size = mesh.shape["row"], mesh.shape["col"]
    chips = row_size // 2
    bins, channels, _ = spectra.shape
    row_index, col_index = lax.axis_index("row"), lax.axis_index("col")
    core = row_index % 2
    ring = [i ^ (i >> 1) for i in range(chips)]
    place = [ring.index(k) for k in range(chips)]
    every = [(r, c) for r in range(row_size) for c in range(col_size)]

    def send(values, moves):
        pairs = [(r * col_size + c, s * col_size + d) for (r, c), (s, d) in moves]
        return lax.ppermute(values, AXES, pairs)

    def along(values, line):
        return send(values, [((r, c), (r, d)) for r in range(row_size) for c, d in line])

    def send_round(values, hop):
        moves = []
        for c in range(col_size):
            for a, way in ((0, 1), (1, -1)):
                here = ring[(place[c] + way * (hop - 1)) % chips]
                there = ring[(place[c] + way * hop) % chips]
                moves.append(((2 * here + a, c), (2 * there + a, c)))
        return send(values, moves)

    def swap_cores(values):
        return send(values, [((r, c), (r ^ 1, c)) for r, c in every])

    outer, inner, out_pass = [(0, 1), (1, 0), (2, 3), (3, 2)], [(1, 2), (2, 1)], [(1, 0), (2, 3)]
    owners = np.array([[0, 1, 2, 3], [1, 0, 2, 3], [2, 3, 1, 0], [3, 2, 1, 0]], np.int32)

    distance = np.zeros((row_size, col_size), np.int32)
    for r, c in every:
        gap = place[r // 2] - place[c]
        distance[r, c] = (gap if r % 2 == 0 else -gap) % chips
    my_distance = jnp.asarray(distance)[row_index, col_index].reshape(1)
    my_owners = jnp.asarray(owners)[col_index]
    at_end = ((col_index == 0) | (col_index == col_size - 1)).astype(jnp.int32).reshape(1)

    n_parts = PARTS
    short = bins // n_parts
    white, *own = whiten_parts(spectra, quality, [bins] + [short] * n_parts)
    row_count = channels * col_size
    col_count = row_count * row_size // col_size
    half_cols = col_count // 2
    norm_scale = 1.0 / math.sqrt(spectra.shape[2] // 2 * bins)
    local_mask = lax.dynamic_slice(
        tile_mask,
        (row_index * (row_count // BLK), col_index * (col_count // BLK)),
        (row_count // BLK, col_count // BLK),
    ).astype(jnp.float32)
    matrices = lag_matrices(bins)
    out_shape = (LAGS, row_count, col_count)
    near_at = core * half_cols + my_owners * channels
    far_at = (1 - core) * half_cols + my_owners * channels
    offsets = jnp.stack([my_owners * channels, near_at, far_at]).astype(jnp.int32)
    tiles = jnp.stack([near_at, far_at], axis=1).reshape(-1) // BLK
    scales = norm_scale * jnp.take(jnp.take(local_mask, my_owners, axis=0), tiles, axis=1)

    rows_of = [list(own)] + [[None] * n_parts for _ in range(1, col_size)]
    near_of = [[None] * n_parts for _ in range(col_size)]
    far_of = [[None] * n_parts for _ in range(col_size)]
    cols_of = [[near_of[j], far_of[j]] for j in range(col_size)]
    out, last = None, own[0]

    def part_of(whole, p):
        return lax.slice_in_dim(whole, p * short, (p + 1) * short, axis=0)

    def take_rows(j, p):
        nonlocal last
        start = p * short
        if j == 2:
            last = pick(at_end, [second_in, second_out], [start, start], short, last)
        else:
            last = pick(at_end, [third_in, third_out[p]], [start, 0], short, last)
            if p + 2 < n_parts:
                third_out[p + 2] = along(part_of(lax.optimization_barrier((third_in, last))[0], p + 2), out_pass)
        rows_of[j][p] = last

    def go_round(j, p):
        nonlocal last
        held = [rows_of[j][p]]
        for hop in range(1, chips):
            held.append(send_round(held[-1], hop))
        last = near_of[j][p] = pick(my_distance, held, [0] * chips, short, last)

    def swap(j):
        for p in range(n_parts):
            far_of[j][p] = swap_cores(near_of[j][p])

    def take_cols(j, p):
        go_round(j, p)
        far_of[j][p] = swap_cores(near_of[j][p])

    def pairs_of(row_sets, col_sets):
        nonlocal out, last
        out, last = correlate(row_sets, col_sets, offsets, scales, rows_of, cols_of, matrices, out, out_shape, last)

    def meet(*values):
        nonlocal last
        values = lax.optimization_barrier((*values, last))
        last = values[-1]
        return values[:-1]

    first, second_in = along(white, outer), along(white, inner)
    for p in range(n_parts):
        go_round(0, p)
    first, second_in, *near_of[0][:] = meet(first, second_in, *near_of[0])

    second_out, third_in = along(second_in, out_pass), along(first, inner)
    swap(0)
    rows_of[1][:] = [part_of(first, p) for p in range(n_parts)]
    pairs_of((1,), (0,))
    pairs_of((0,), (0,))
    for p in range(n_parts):
        go_round(1, p)
    second_in, second_out, third_in, out, *near_of[1][:] = meet(second_in, second_out, third_in, out, *near_of[1])

    third_out = [along(part_of(third_in, p), out_pass) for p in range(2)] + [None] * (n_parts - 2)
    swap(1)
    for p in range(n_parts):
        take_rows(2, p)
    pairs_of((0, 1), (1,))
    take_rows(3, 0)
    pairs_of((2,), (0, 1))
    take_rows(3, 1)
    take_cols(2, 0)
    take_cols(2, 1)
    take_rows(3, 2)
    take_cols(2, 2)
    take_cols(2, 3)
    take_cols(3, 0)
    take_rows(3, 3)
    take_cols(3, 1)
    pairs_of((0, 1, 2), (2,))
    take_cols(3, 2)
    pairs_of((3,), (0, 1, 2))
    take_cols(3, 3)
    pairs_of((0, 1, 2, 3), (3,))
    return out


def solution(mesh):
    def per_device(spectra, quality, tile_mask):
        row_size, col_size = mesh.shape["row"], mesh.shape["col"]
        fits = col_size == 4 and row_size == 2 * col_size and spectra.shape[1] == BLK
        fits = fits and spectra.shape[0] % (PARTS * STEP_BINS) == 0
        plan = line_plan if fits else general_plan
        return plan(mesh, spectra, quality, tile_mask)

    placed = (P(None, AXES, None), P(AXES), P())
    return jax.shard_map(
        per_device, mesh=mesh, in_specs=placed, out_specs=P(None, "row", "col"), check_vma=False
    )
```

time: 648 us -> 505 us (0.78)
  starting transfers between devices: 201 us -> 102 us
  Pallas kernels: 287 us -> 190 us
  waiting for transfers between devices: 133 us -> 186 us
    ppermute x88 -> x72, starting transfers between devices: 201 us -> 102 us  [send(): return lax.ppermute(values, AXES, pairs)]
    pallas_call x32 -> x31, Pallas kernels: 280 us -> 182 us  [the longest x7 123 us: correlate(): pl.pallas_call(functools.partial(correlate_kernel, row_sets, col_sets, x_...]
    ppermute x88 -> x72, waiting for transfers between devices: 133 us -> 186 us  [send(): return lax.ppermute(values, AXES, pairs)]
    slice x0 -> x4, local copies, waits for them, and re-layouts: none -> 9.25 us  [part_of(): return lax.slice_in_dim(whole, p * short, (p + 1) * short, axis=0)]
    gather x12 -> x3, local copies, waits for them, and re-layouts: 7.92 us -> 1.19 us  [the longest x2 0.64 us: line_plan(): jnp.take(jnp.take(local_mask, my_owners, axis=0), tiles, axis=1)]
  transfers between devices with their start and end apart: 88 -> 72, of which waited for: 17 -> 20; matrix products, arithmetic and copies ran while one was open for 2% -> 3% of each run, Pallas kernels for 32% -> 31%
where the time goes in v2:
time: 505 us; the launch traced here: 503 us
  Pallas kernels  190 us (38%)
  waiting for transfers between devices  186 us (37%)
  starting transfers between devices  102 us (20%)
  local copies, waits for them, and re-layouts  21.4 us (4%)
    ppermute x72, waiting for transfers between devices, send(): return lax.ppermute(values, AXES, pairs)  186 us
    pallas_call x7, Pallas kernels, correlate(): pl.pallas_call(functools.partial(correlate_kernel, row_sets, col_sets, x_...  123 us
    ppermute x72, starting transfers between devices, send(): return lax.ppermute(values, AXES, pairs)  102 us
    pallas_call x24, Pallas kernels, pick(): pl.pallas_call(functools.partial(pick_kernel, tuple(starts)), grid_spec=p...  58.7 us
  transfers between devices with their start and end apart: 72, of which 20 were waited for; matrix products, arithmetic and copies ran while one was open for 3% of the time, Pallas kernels for 31%

profile of v2, /device:TPU:7, one launch (start us, length us, event | category | flops | bytes accessed | tf_op | source)
XLA Modules:
  0.0 502.6 jit_solution(16396233100159531606)
XLA Ops:
  1.4 8.2 %whiten.1 = (bf16[32,128,512]{2,1,0:T(8,128)(2,1)}, bf16[8,128,512]{2,1,0:T(8,128)(2,1)}, bf16[8,128,512]{2,1,0:T(8,128)(2,1)}, bf16[8,128,512]{2,1,0:T(8,128)(2,1)}, bf16[8,128,512]{2,1,0:T(8,128)(2,1)}) custom-call(bf16[32,128,512]{2,1,0:T(8,128)(2,1)} %spectra_ref.1, s32[128,1]{1,0:T(8,128)} %copy.23.quality_ref), custom_call_target="tpu_custom_call" | custom-call | tf_op jit(solution)/shard_map/whiten/pallas_call | solution.py:108
  20.5 30.6 %collective-permute-done.3.refs_2_ = bf16[8,128,512]{2,1,0:T(8,128)(2,1)S(1)} collective-permute-done((bf16[8,128,512]{2,1,0:T(8,128)(2,1)S(1)}, bf16[8,128,512]{2,1,0:T(8,128)(2,1)S(1)}, u32[]{:S(2)}, u32[]{:S(2)}) %collective-permute-start.3) | collective-permute-done | bytes 1048608 | tf_op jit(solution)/shard_map/ppermute | solution.py:408
  52.4 9.9 %collective-permute-done.6.refs_2_ = bf16[8,128,512]{2,1,0:T(8,128)(2,1)} collective-permute-done((bf16[8,128,512]{2,1,0:T(8,128)(2,1)S(1)}, bf16[8,128,512]{2,1,0:T(8,128)(2,1)}, u32[]{:S(2)}, u32[]{:S(2)}) %collective-permute-start.6) | collective-permute-done | bytes 1048608 | tf_op jit(solution)/shard_map/ppermute | solution.py:408
  63.7 9.9 %collective-permute-done.9.refs_2_ = bf16[8,128,512]{2,1,0:T(8,128)(2,1)} collective-permute-done((bf16[8,128,512]{2,1,0:T(8,128)(2,1)S(1)}, bf16[8,128,512]{2,1,0:T(8,128)(2,1)}, u32[]{:S(2)}, u32[]{:S(2)}) %collective-permute-start.9) | collective-permute-done | bytes 1048608 | tf_op jit(solution)/shard_map/ppermute | solution.py:408
  75.8 8.9 %collective-permute-done.12.refs_2_ = bf16[8,128,512]{2,1,0:T(8,128)(2,1)} collective-permute-done((bf16[8,128,512]{2,1,0:T(8,128)(2,1)S(1)}, bf16[8,128,512]{2,1,0:T(8,128)(2,1)}, u32[]{:S(2)}, u32[]{:S(2)}) %collective-permute-start.12) | collective-permute-done | bytes 1048608 | tf_op jit(solution)/shard_map/ppermute | solution.py:408
  100.8 8.5 %collective-permute-done.13.refs_3_ = bf16[8,128,512]{2,1,0:T(8,128)(2,1)} collective-permute-done((bf16[8,128,512]{2,1,0:T(8,128)(2,1)}, bf16[8,128,512]{2,1,0:T(8,128)(2,1)}, u32[]{:S(2)}, u32[]{:S(2)}) %collective-permute-start.13) | collective-permute-done | bytes 1048608 | tf_op jit(solution)/shard_map/ppermute | solution.py:408
  131.1 30.0 %collective-permute-done.21.refs_2_ = bf16[8,128,512]{2,1,0:T(8,128)(2,1)} collective-permute-done((bf16[8,128,512]{2,1,0:T(8,128)(2,1)S(1)}, bf16[8,128,512]{2,1,0:T(8,128)(2,1)}, u32[]{:S(2)}, u32[]{:S(2)}) %collective-permute-start.21) | collective-permute-done | bytes 1048608 | tf_op jit(solution)/shard_map/ppermute | solution.py:408
  162.4 9.9 %collective-permute-done.24.refs_2_ = bf16[8,128,512]{2,1,0:T(8,128)(2,1)S(1)} collective-permute-done((bf16[8,128,512]{2,1,0:T(8,128)(2,1)S(1)}, bf16[8,128,512]{2,1,0:T(8,128)(2,1)S(1)}, u32[]{:S(2)}, u32[]{:S(2)}) %collective-permute-start.24) | collective-permute-done | bytes 1048608 | tf_op jit(solution)/shard_map/ppermute | solution.py:408
  177.1 6.7 %collective-permute-done.27.refs_2_ = bf16[8,128,512]{2,1,0:T(8,128)(2,1)} collective-permute-done((bf16[8,128,512]{2,1,0:T(8,128)(2,1)}, bf16[8,128,512]{2,1,0:T(8,128)(2,1)}, u32[]{:S(2)}, u32[]{:S(2)}) %collective-permute-start.27) | collective-permute-done | bytes 1048608 | tf_op jit(solution)/shard_map/ppermute | solution.py:408
  186.1 9.0 %collective-permute-done.30.refs_2_ = bf16[8,128,512]{2,1,0:T(8,128)(2,1)} collective-permute-done((bf16[8,128,512]{2,1,0:T(8,128)(2,1)}, bf16[8,128,512]{2,1,0:T(8,128)(2,1)}, u32[]{:S(2)}, u32[]{:S(2)}) %collective-permute-start.30) | collective-permute-done | bytes 1048608 | tf_op jit(solution)/shard_map/ppermute | solution.py:408
  201.9 10.7 %correlate.7 = (bf16[64,512,1024]{2,1,0:T(8,128)(2,1)}, s32[8,128]{1,0:T(8,128)}) custom-call(s32[3,4]{1,0:T(4,128)} %pad_add_fusion.offset_ref, f32[4,8]{1,0:T(4,128)} %multiply_bitcast_fusion.scale_ref, bf16[8,128,512]{2,1,0:T(8,128)(2,1)} %copy-done.7, bf16[8,128,512]{2,1,0:T(8,128)(2,1)} %copy-done.6, bf16[8,128,512]{2,1,0:T(8,128)(2,1)} %copy-done.5, ...), custom_call_target="tpu_custom_call" | custom-call | bytes 1024 | tf_op jit(solution)/shard_map/correlate/pallas_call | solution.py:358
  212.6 10.7 %correlate.8 = (bf16[64,512,1024]{2,1,0:T(8,128)(2,1)}, s32[8,128]{1,0:T(8,128)}) custom-call(s32[3,4]{1,0:T(4,128)} %pad_add_fusion.offset_ref, f32[4,8]{1,0:T(4,128)} %multiply_bitcast_fusion.scale_ref, bf16[8,128,512]{2,1,0:T(8,128)(2,1)} %get-tuple-element.41.refs_0_.refs_4_, ...), custom_call_target="tpu_custom_call", output_to_operand_aliasing={{0}: (16, {})} | custom-call | bytes 1024 | tf_op jit(solution)/shard_map/correlate/pallas_call | solution.py:358
  252.5 16.0 %correlate.9 = (bf16[64,512,1024]{2,1,0:T(8,128)(2,1)}, s32[8,128]{1,0:T(8,128)}) custom-call(s32[3,4]{1,0:T(4,128)} %pad_add_fusion.offset_ref, f32[4,8]{1,0:T(4,128)} %multiply_bitcast_fusion.scale_ref, bf16[8,128,512]{2,1,0:T(8,128)(2,1)} %get-tuple-element.41.refs_0_.refs_4_, ...), custom_call_target="tpu_custom_call", output_to_operand_aliasing={{0}: (20, {})} | custom-call | bytes 1024 | tf_op jit(solution)/shard_map/correlate/pallas_call | solution.py:358
  276.1 11.5 %collective-permute-done.37.refs_1_ = bf16[8,128,512]{2,1,0:T(8,128)(2,1)} collective-permute-done((bf16[8,128,512]{2,1,0:T(8,128)(2,1)}, bf16[8,128,512]{2,1,0:T(8,128)(2,1)}, u32[]{:S(2)}, u32[]{:S(2)}) %collective-permute-start.37) | collective-permute-done | bytes 1048608 | tf_op jit(solution)/shard_map/ppermute | solution.py:408
  292.3 7.3 %collective-permute-done.40.refs_2_ = bf16[8,128,512]{2,1,0:T(8,128)(2,1)} collective-permute-done((bf16[8,128,512]{2,1,0:T(8,128)(2,1)S(1)}, bf16[8,128,512]{2,1,0:T(8,128)(2,1)}, u32[]{:S(2)}, u32[]{:S(2)}) %collective-permute-start.40) | collective-permute-done | bytes 1048608 | tf_op jit(solution)/shard_map/ppermute | solution.py:408
  303.1 11.1 %collective-permute-done.38.refs_1_ = bf16[8,128,512]{2,1,0:T(8,128)(2,1)S(1)} collective-permute-done((bf16[8,128,512]{2,1,0:T(8,128)(2,1)S(1)}, bf16[8,128,512]{2,1,0:T(8,128)(2,1)S(1)}, u32[]{:S(2)}, u32[]{:S(2)}) %collective-permute-start.38) | collective-permute-done | bytes 1048608 | tf_op jit(solution)/shard_map/ppermute | solution.py:408
  317.5 16.6 %correlate.10 = (bf16[64,512,1024]{2,1,0:T(8,128)(2,1)}, s32[8,128]{1,0:T(8,128)}) custom-call(s32[3,4]{1,0:T(4,128)} %pad_add_fusion.offset_ref, f32[4,8]{1,0:T(4,128)} %multiply_bitcast_fusion.scale_ref, bf16[8,128,512]{2,1,0:T(8,128)(2,1)} %pick.32.refs_2_.refs_0_.refs_8_, ...), custom_call_target="tpu_custom_call", output_to_operand_aliasing={{0}: (24, {})} | custom-call | bytes 1024 | tf_op jit(solution)/shard_map/correlate/pallas_call | solution.py:358
  365.7 7.6 %collective-permute-done.48.refs_3_ = bf16[8,128,512]{2,1,0:T(8,128)(2,1)S(1)} collective-permute-done((bf16[8,128,512]{2,1,0:T(8,128)(2,1)}, bf16[8,128,512]{2,1,0:T(8,128)(2,1)S(1)}, u32[]{:S(2)}, u32[]{:S(2)}) %collective-permute-start.48) | collective-permute-done | bytes 1048608 | tf_op jit(solution)/shard_map/ppermute | solution.py:408
  391.6 4.7 collective-permute-done.57.refs_3_
  396.3 5.1 %collective-permute-start.62 = (bf16[8,128,512]{2,1,0:T(8,128)(2,1)S(1)}, bf16[8,128,512]{2,1,0:T(8,128)(2,1)}, u32[]{:S(2)}, u32[]{:S(2)}) collective-permute-start(bf16[8,128,512]{2,1,0:T(8,128)(2,1)S(1)} %copy-done.19), channel_id=1, source_target_pairs={{0,4},{1,5},{2,6},{3,7},{4,0},{5,1},{6,2},{7,3},{8,12},{9,13},{10,... | collective-permute-start | bytes 3145736 | tf_op jit(solution)/shard_map/ppermute | solution.py:408
  407.4 8.9 %collective-permute-done.66.refs_2_ = bf16[8,128,512]{2,1,0:T(8,128)(2,1)} collective-permute-done((bf16[8,128,512]{2,1,0:T(8,128)(2,1)S(1)}, bf16[8,128,512]{2,1,0:T(8,128)(2,1)}, u32[]{:S(2)}, u32[]{:S(2)}) %collective-permute-start.66) | collective-permute-done | bytes 1048608 | tf_op jit(solution)/shard_map/ppermute | solution.py:408
  423.3 20.9 %correlate.11 = (bf16[64,512,1024]{2,1,0:T(8,128)(2,1)}, s32[8,128]{1,0:T(8,128)}) custom-call(s32[3,4]{1,0:T(4,128)} %pad_add_fusion.offset_ref, f32[4,8]{1,0:T(4,128)} %multiply_bitcast_fusion.scale_ref, bf16[8,128,512]{2,1,0:T(8,128)(2,1)} %get-tuple-element.41.refs_0_.refs_4_, ...), custom_call_target="tpu_custom_call", output_to_operand_aliasing={{0}: (24, {})} | custom-call | bytes 1024 | tf_op jit(solution)/shard_map/correlate/pallas_call | solution.py:358
  447.3 22.5 %correlate.12 = (bf16[64,512,1024]{2,1,0:T(8,128)(2,1)}, s32[8,128]{1,0:T(8,128)}) custom-call(s32[3,4]{1,0:T(4,128)} %pad_add_fusion.offset_ref, f32[4,8]{1,0:T(4,128)} %multiply_bitcast_fusion.scale_ref, bf16[8,128,512]{2,1,0:T(8,128)(2,1)} %pick.36.refs_23_.refs_0_.refs_12_, ...), custom_call_target="tpu_custom_call", output_to_operand_aliasing={{0}: (32, {})} | custom-call | bytes 1024 | tf_op jit(solution)/shard_map/correlate/pallas_call | solution.py:358
  476.4 26.0 %correlate.13 = (bf16[64,512,1024]{2,1,0:T(8,128)(2,1)}, s32[8,128]{1,0:T(8,128)}) custom-call(s32[3,4]{1,0:T(4,128)} %pad_add_fusion.offset_ref, f32[4,8]{1,0:T(4,128)} %multiply_bitcast_fusion.scale_ref, bf16[8,128,512]{2,1,0:T(8,128)(2,1)} %get-tuple-element.41.refs_0_.refs_4_, ...), custom_call_target="tpu_custom_call", output_to_operand_aliasing={{0}: (28, {})} | custom-call | bytes 1024 | tf_op jit(solution)/shard_map/correlate/pallas_call | solution.py:358
  (275 shorter events, 189.9 us)
Async XLA Ops:
  11.8 100.2 %collective-permute-start = (bf16[32,128,512]{2,1,0:T(8,128)(2,1)}, bf16[32,128,512]{2,1,0:T(8,128)(2,1)}, u32[]{:S(2)}, u32[]{:S(2)}) collective-permute-start(bf16[32,128,512]{2,1,0:T(8,128)(2,1)} %get-tuple-element.45), channel_id=1, source_target_pairs={{0,1},{1,0},{2,3},{3,2},{4,5},{5,4},{6,7},{7,6},{8,9},{9,8},{10,11... | collective-permute-start | bytes 12582920 | tf_op jit(solution)/shard_map/ppermute | solution.py:408
  13.2 98.9 %collective-permute-start.1 = (bf16[32,128,512]{2,1,0:T(8,128)(2,1)}, bf16[32,128,512]{2,1,0:T(8,128)(2,1)}, u32[]{:S(2)}, u32[]{:S(2)}) collective-permute-start(bf16[32,128,512]{2,1,0:T(8,128)(2,1)} %get-tuple-element.45), channel_id=1, source_target_pairs={{1,2},{2,1},{5,6},{6,5},{9,10},{10,9},{13,14},{14,13},{17,18},{18,... | collective-permute-start | bytes 12582920 | tf_op jit(solution)/shard_map/ppermute | solution.py:408
  16.6 34.5 %collective-permute-start.3 = (bf16[8,128,512]{2,1,0:T(8,128)(2,1)S(1)}, bf16[8,128,512]{2,1,0:T(8,128)(2,1)S(1)}, u32[]{:S(2)}, u32[]{:S(2)}) collective-permute-start(bf16[8,128,512]{2,1,0:T(8,128)(2,1)S(1)} %collective-permute-done.2.refs_1_), channel_id=1, source_target_pairs={{8,24},{20,28},{25,17},{5,21},{2,10},{30,14},{19,3},{15,7}} | collective-permute-start | bytes 3145736 | tf_op jit(solution)/shard_map/ppermute | solution.py:408
  17.9 44.4 %collective-permute-start.6 = (bf16[8,128,512]{2,1,0:T(8,128)(2,1)S(1)}, bf16[8,128,512]{2,1,0:T(8,128)(2,1)}, u32[]{:S(2)}, u32[]{:S(2)}) collective-permute-start(bf16[8,128,512]{2,1,0:T(8,128)(2,1)S(1)} %collective-permute-done.5.refs_1_), channel_id=1, source_target_pairs={{8,24},{20,28},{25,17},{5,21},{2,10},{30,14},{19,3},{15,7}} | collective-permute-start | bytes 3145736 | tf_op jit(solution)/shard_map/ppermute | solution.py:408
  19.2 54.3 %collective-permute-start.9 = (bf16[8,128,512]{2,1,0:T(8,128)(2,1)S(1)}, bf16[8,128,512]{2,1,0:T(8,128)(2,1)}, u32[]{:S(2)}, u32[]{:S(2)}) collective-permute-start(bf16[8,128,512]{2,1,0:T(8,128)(2,1)S(1)} %collective-permute-done.8.refs_1_), channel_id=1, source_target_pairs={{8,24},{20,28},{25,17},{5,21},{2,10},{30,14},{19,3},{15,7}} | collective-permute-start | bytes 3145736 | tf_op jit(solution)/shard_map/ppermute | solution.py:408
  121.5 112.5 %collective-permute-start.14 = (bf16[32,128,512]{2,1,0:T(8,128)(2,1)}, bf16[32,128,512]{2,1,0:T(8,128)(2,1)}, u32[]{:S(2)}, u32[]{:S(2)}) collective-permute-start(bf16[32,128,512]{2,1,0:T(8,128)(2,1)} %collective-permute-done.1.refs_0_), channel_id=1, source_target_pairs={{1,0},{2,3},{5,4},{6,7},{9,8},{10,11},{13,12},{14,15},{17,16},{18,... | collective-permute-start | bytes 12582920 | tf_op jit(solution)/shard_map/ppermute | solution.py:408
  122.8 111.2 %collective-permute-start.15 = (bf16[32,128,512]{2,1,0:T(8,128)(2,1)}, bf16[32,128,512]{2,1,0:T(8,128)(2,1)}, u32[]{:S(2)}, u32[]{:S(2)}) collective-permute-start(bf16[32,128,512]{2,1,0:T(8,128)(2,1)} %collective-permute-done), channel_id=1, source_target_pairs={{1,2},{2,1},{5,6},{6,5},{9,10},{10,9},{13,14},{14,13},{17,18},{18,... | collective-permute-start | bytes 12582920 | tf_op jit(solution)/shard_map/ppermute | solution.py:408
  127.2 33.9 %collective-permute-start.21 = (bf16[8,128,512]{2,1,0:T(8,128)(2,1)S(1)}, bf16[8,128,512]{2,1,0:T(8,128)(2,1)}, u32[]{:S(2)}, u32[]{:S(2)}) collective-permute-start(bf16[8,128,512]{2,1,0:T(8,128)(2,1)S(1)} %collective-permute-done.20.refs_1_), channel_id=1, source_target_pairs={{8,24},{20,28},{25,17},{5,21},{2,10},{30,14},{19,3},{15,7}} | collective-permute-start | bytes 3145736 | tf_op jit(solution)/shard_map/ppermute | solution.py:408
  128.5 43.8 %collective-permute-start.24 = (bf16[8,128,512]{2,1,0:T(8,128)(2,1)S(1)}, bf16[8,128,512]{2,1,0:T(8,128)(2,1)S(1)}, u32[]{:S(2)}, u32[]{:S(2)}) collective-permute-start(bf16[8,128,512]{2,1,0:T(8,128)(2,1)S(1)} %collective-permute-done.23.refs_1_), channel_id=1, source_target_pairs={{8,24},{20,28},{25,17},{5,21},{2,10},{30,14},{19,3},{15,7}} | collective-permute-start | bytes 3145736 | tf_op jit(solution)/shard_map/ppermute | solution.py:408
  129.8 54.0 %collective-permute-start.27 = (bf16[8,128,512]{2,1,0:T(8,128)(2,1)}, bf16[8,128,512]{2,1,0:T(8,128)(2,1)}, u32[]{:S(2)}, u32[]{:S(2)}) collective-permute-start(bf16[8,128,512]{2,1,0:T(8,128)(2,1)} %collective-permute-done.26.refs_1_), channel_id=1, source_target_pairs={{8,24},{20,28},{25,17},{5,21},{2,10},{30,14},{19,3},{15,7}} | collective-permute-start | bytes 3145736 | tf_op jit(solution)/shard_map/ppermute | solution.py:408
  161.1 33.9 %collective-permute-start.30 = (bf16[8,128,512]{2,1,0:T(8,128)(2,1)}, bf16[8,128,512]{2,1,0:T(8,128)(2,1)}, u32[]{:S(2)}, u32[]{:S(2)}) collective-permute-start(bf16[8,128,512]{2,1,0:T(8,128)(2,1)} %collective-permute-done.29.refs_1_), channel_id=1, source_target_pairs={{8,24},{20,28},{25,17},{5,21},{2,10},{30,14},{19,3},{15,7}} | collective-permute-start | bytes 3145736 | tf_op jit(solution)/shard_map/ppermute | solution.py:408
  183.8 42.1 %collective-permute-start.25 = (bf16[8,128,512]{2,1,0:T(8,128)(2,1)}, bf16[8,128,512]{2,1,0:T(8,128)(2,1)}, u32[]{:S(2)}, u32[]{:S(2)}) collective-permute-start(bf16[8,128,512]{2,1,0:T(8,128)(2,1)} %copy-done.29), channel_id=1, source_target_pairs={{24,16},{28,12},{17,1},{21,29},{10,26},{14,6},{3,11},{7,23}} | collective-permute-start | bytes 3145736 | tf_op jit(solution)/shard_map/ppermute | solution.py:408
  197.3 34.0 %collective-permute-start.31 = (bf16[8,128,512]{2,1,0:T(8,128)(2,1)}, bf16[8,128,512]{2,1,0:T(8,128)(2,1)}, u32[]{:S(2)}, u32[]{:S(2)}) collective-permute-start(bf16[8,128,512]{2,1,0:T(8,128)(2,1)} %collective-permute-done.30.refs_2_), channel_id=1, source_target_pairs={{24,16},{28,12},{17,1},{21,29},{10,26},{14,6},{3,11},{7,23}} | collective-permute-start | bytes 3145736 | tf_op jit(solution)/shard_map/ppermute | solution.py:408
  248.3 39.3 %collective-permute-start.37 = (bf16[8,128,512]{2,1,0:T(8,128)(2,1)}, bf16[8,128,512]{2,1,0:T(8,128)(2,1)}, u32[]{:S(2)}, u32[]{:S(2)}) collective-permute-start(bf16[8,128,512]{2,1,0:T(8,128)(2,1)} %get-tuple-element.77), channel_id=1, source_target_pairs={{1,0},{2,3},{5,4},{6,7},{9,8},{10,11},{13,12},{14,15},{17,16},{18,... | collective-permute-start | bytes 3145736 | tf_op jit(solution)/shard_map/ppermute | solution.py:408
  249.6 38.7 %collective-permute-start.52 = (bf16[8,128,512]{2,1,0:T(8,128)(2,1)}, bf16[8,128,512]{2,1,0:T(8,128)(2,1)S(1)}, u32[]{:S(2)}, u32[]{:S(2)}) collective-permute-start(bf16[8,128,512]{2,1,0:T(8,128)(2,1)} %pick.34.refs_2_.refs_0_.refs_10_), channel_id=1, source_target_pairs={{0,8},{4,20},{9,25},{13,5},{18,2},{22,30},{27,19},{31,15}} | collective-permute-start | bytes 3145736 | tf_op jit(solution)/shard_map/ppermute | solution.py:408
  289.7 46.4 %collective-permute-start.53 = (bf16[8,128,512]{2,1,0:T(8,128)(2,1)S(1)}, bf16[8,128,512]{2,1,0:T(8,128)(2,1)S(1)}, u32[]{:S(2)}, u32[]{:S(2)}) collective-permute-start(bf16[8,128,512]{2,1,0:T(8,128)(2,1)S(1)} %collective-permute-done.52.refs_1_), channel_id=1, source_target_pairs={{8,24},{20,28},{25,17},{5,21},{2,10},{30,14},{19,3},{15,7}} | collective-permute-start | bytes 3145736 | tf_op jit(solution)/shard_map/ppermute | solution.py:408
  291.0 46.8 %collective-permute-start.50 = (bf16[8,128,512]{2,1,0:T(8,128)(2,1)}, bf16[8,128,512]{2,1,0:T(8,128)(2,1)}, u32[]{:S(2)}, u32[]{:S(2)}) collective-permute-start(bf16[8,128,512]{2,1,0:T(8,128)(2,1)} %collective-permute-done.49.refs_1_), channel_id=1, source_target_pairs={{8,24},{20,28},{25,17},{5,21},{2,10},{30,14},{19,3},{15,7}} | collective-permute-start | bytes 3145736 | tf_op jit(solution)/shard_map/ppermute | solution.py:408
  299.6 41.8 %collective-permute-start.44 = (bf16[8,128,512]{2,1,0:T(8,128)(2,1)S(1)}, bf16[8,128,512]{2,1,0:T(8,128)(2,1)}, u32[]{:S(2)}, u32[]{:S(2)}) collective-permute-start(bf16[8,128,512]{2,1,0:T(8,128)(2,1)S(1)} %collective-permute-done.43.refs_2_), channel_id=1, source_target_pairs={{24,16},{28,12},{17,1},{21,29},{10,26},{14,6},{3,11},{7,23}} | collective-permute-start | bytes 3145736 | tf_op jit(solution)/shard_map/ppermute | solution.py:408
  301.8 40.9 %collective-permute-start.47 = (bf16[8,128,512]{2,1,0:T(8,128)(2,1)S(1)}, bf16[8,128,512]{2,1,0:T(8,128)(2,1)}, u32[]{:S(2)}, u32[]{:S(2)}) collective-permute-start(bf16[8,128,512]{2,1,0:T(8,128)(2,1)S(1)} %collective-permute-done.46.refs_1_), channel_id=1, source_target_pairs={{8,24},{20,28},{25,17},{5,21},{2,10},{30,14},{19,3},{15,7}} | collective-permute-start | bytes 3145736 | tf_op jit(solution)/shard_map/ppermute | solution.py:408
  354.1 34.8 %collective-permute-start.58 = (bf16[8,128,512]{2,1,0:T(8,128)(2,1)}, bf16[8,128,512]{2,1,0:T(8,128)(2,1)}, u32[]{:S(2)}, u32[]{:S(2)}) collective-permute-start(bf16[8,128,512]{2,1,0:T(8,128)(2,1)} %pick.40.refs_4_.refs_0_.refs_2_.refs_14_), channel_id=1, source_target_pairs={{0,8},{4,20},{9,25},{13,5},{18,2},{22,30},{27,19},{31,15}} | collective-permute-start | bytes 3145736 | tf_op jit(solution)/shard_map/ppermute | solution.py:408
  405.0 39.2 %collective-permute-start.60 = (bf16[8,128,512]{2,1,0:T(8,128)(2,1)}, bf16[8,128,512]{2,1,0:T(8,128)(2,1)}, u32[]{:S(2)}, u32[]{:S(2)}) collective-permute-start(bf16[8,128,512]{2,1,0:T(8,128)(2,1)} %collective-permute-done.59.refs_2_), channel_id=1, source_target_pairs={{24,16},{28,12},{17,1},{21,29},{10,26},{14,6},{3,11},{7,23}} | collective-permute-start | bytes 3145736 | tf_op jit(solution)/shard_map/ppermute | solution.py:408
  416.3 53.6 %collective-permute-start.67 = (bf16[8,128,512]{2,1,0:T(8,128)(2,1)}, bf16[8,128,512]{2,1,0:T(8,128)(2,1)}, u32[]{:S(2)}, u32[]{:S(2)}) collective-permute-start(bf16[8,128,512]{2,1,0:T(8,128)(2,1)} %collective-permute-done.66.refs_2_), channel_id=1, source_target_pairs={{24,16},{28,12},{17,1},{21,29},{10,26},{14,6},{3,11},{7,23}} | collective-permute-start | bytes 3145736 | tf_op jit(solution)/shard_map/ppermute | solution.py:408
  421.3 51.4 %collective-permute-start.68 = (bf16[8,128,512]{2,1,0:T(8,128)(2,1)S(1)}, bf16[8,128,512]{2,1,0:T(8,128)(2,1)S(1)}, u32[]{:S(2)}, u32[]{:S(2)}) collective-permute-start(bf16[8,128,512]{2,1,0:T(8,128)(2,1)S(1)} %copy-done.21), channel_id=1, source_target_pairs={{0,4},{1,5},{2,6},{3,7},{4,0},{5,1},{6,2},{7,3},{8,12},{9,13},{10,... | collective-permute-start | bytes 3145736 | tf_op jit(solution)/shard_map/ppermute | solution.py:408
  422.2 50.4 %collective-permute-start.69 = (bf16[8,128,512]{2,1,0:T(8,128)(2,1)}, bf16[8,128,512]{2,1,0:T(8,128)(2,1)S(1)}, u32[]{:S(2)}, u32[]{:S(2)}) collective-permute-start(bf16[8,128,512]{2,1,0:T(8,128)(2,1)} %pick.45.refs_23_.refs_17_), channel_id=1, source_target_pairs={{0,4},{1,5},{2,6},{3,7},{4,0},{5,1},{6,2},{7,3},{8,12},{9,13},{10,... | collective-permute-start | bytes 3145736 | tf_op jit(solution)/shard_map/ppermute | solution.py:408
  (97 other events, 2119.6 us)

commit v3 on v2

--- a/solution.py
+++ b/solution.py
@@ -16,7 +16,7 @@
 GROUP = 8
 VMEM_BYTES = 58 * 1024 * 1024
 AXES = ("row", "col")
-DEPTH = 3
+DEPTH = 5
 LIGHT = pl.CostEstimate(flops=0, bytes_accessed=1024, transcendentals=0)
 TOKEN = jax.ShapeDtypeStruct((8, 128), jnp.int32)
 

time: 505 us -> 496 us (0.982)
  Pallas kernels: 190 us -> 180 us
    pallas_call x7, Pallas kernels: 123 us -> 113 us  [correlate(): pl.pallas_call(functools.partial(correlate_kernel, row_sets, col_sets, x_...]
  transfers between devices with their start and end apart: 72 -> 72, of which waited for: 20 -> 20; matrix products, arithmetic and copies ran while one was open for 3% -> 3% of each run, Pallas kernels for 31% -> 30%
where the time goes in v3:
time: 496 us; the launch traced here: 493 us
  waiting for transfers between devices  186 us (38%)
  Pallas kernels  180 us (36%)
  starting transfers between devices  102 us (21%)
  local copies, waits for them, and re-layouts  21.4 us (4%)
    ppermute x72, waiting for transfers between devices, send(): return lax.ppermute(values, AXES, pairs)  186 us
    pallas_call x7, Pallas kernels, correlate(): pl.pallas_call(functools.partial(correlate_kernel, row_sets, col_sets, x_...  113 us
    ppermute x72, starting transfers between devices, send(): return lax.ppermute(values, AXES, pairs)  102 us
    pallas_call x24, Pallas kernels, pick(): pl.pallas_call(functools.partial(pick_kernel, tuple(starts)), grid_spec=p...  58.7 us
  transfers between devices with their start and end apart: 72, of which 20 were waited for; matrix products, arithmetic and copies ran while one was open for 3% of the time, Pallas kernels for 30%

profile of v3, /device:TPU:7, one launch (start us, length us, event | category | flops | bytes accessed | tf_op | source)
XLA Modules:
  0.0 493.5 jit_solution(6457098911375094786)
XLA Ops:
  1.4 8.2 %whiten.1 = (bf16[32,128,512]{2,1,0:T(8,128)(2,1)}, bf16[8,128,512]{2,1,0:T(8,128)(2,1)}, bf16[8,128,512]{2,1,0:T(8,128)(2,1)}, bf16[8,128,512]{2,1,0:T(8,128)(2,1)}, bf16[8,128,512]{2,1,0:T(8,128)(2,1)}) custom-call(bf16[32,128,512]{2,1,0:T(8,128)(2,1)} %spectra_ref.1, s32[128,1]{1,0:T(8,128)} %copy.23.quality_ref), custom_call_target="tpu_custom_call" | custom-call | tf_op jit(solution)/shard_map/whiten/pallas_call | solution.py:108
  20.5 30.6 %collective-permute-done.3.refs_2_ = bf16[8,128,512]{2,1,0:T(8,128)(2,1)S(1)} collective-permute-done((bf16[8,128,512]{2,1,0:T(8,128)(2,1)S(1)}, bf16[8,128,512]{2,1,0:T(8,128)(2,1)S(1)}, u32[]{:S(2)}, u32[]{:S(2)}) %collective-permute-start.3) | collective-permute-done | bytes 1048608 | tf_op jit(solution)/shard_map/ppermute | solution.py:408
  52.4 9.9 %collective-permute-done.6.refs_2_ = bf16[8,128,512]{2,1,0:T(8,128)(2,1)} collective-permute-done((bf16[8,128,512]{2,1,0:T(8,128)(2,1)S(1)}, bf16[8,128,512]{2,1,0:T(8,128)(2,1)}, u32[]{:S(2)}, u32[]{:S(2)}) %collective-permute-start.6) | collective-permute-done | bytes 1048608 | tf_op jit(solution)/shard_map/ppermute | solution.py:408
  63.7 9.9 %collective-permute-done.9.refs_2_ = bf16[8,128,512]{2,1,0:T(8,128)(2,1)} collective-permute-done((bf16[8,128,512]{2,1,0:T(8,128)(2,1)S(1)}, bf16[8,128,512]{2,1,0:T(8,128)(2,1)}, u32[]{:S(2)}, u32[]{:S(2)}) %collective-permute-start.9) | collective-permute-done | bytes 1048608 | tf_op jit(solution)/shard_map/ppermute | solution.py:408
  75.8 8.9 %collective-permute-done.12.refs_2_ = bf16[8,128,512]{2,1,0:T(8,128)(2,1)} collective-permute-done((bf16[8,128,512]{2,1,0:T(8,128)(2,1)S(1)}, bf16[8,128,512]{2,1,0:T(8,128)(2,1)}, u32[]{:S(2)}, u32[]{:S(2)}) %collective-permute-start.12) | collective-permute-done | bytes 1048608 | tf_op jit(solution)/shard_map/ppermute | solution.py:408
  100.8 8.5 %collective-permute-done.13.refs_3_ = bf16[8,128,512]{2,1,0:T(8,128)(2,1)} collective-permute-done((bf16[8,128,512]{2,1,0:T(8,128)(2,1)}, bf16[8,128,512]{2,1,0:T(8,128)(2,1)}, u32[]{:S(2)}, u32[]{:S(2)}) %collective-permute-start.13) | collective-permute-done | bytes 1048608 | tf_op jit(solution)/shard_map/ppermute | solution.py:408
  131.1 30.0 %collective-permute-done.21.refs_2_ = bf16[8,128,512]{2,1,0:T(8,128)(2,1)} collective-permute-done((bf16[8,128,512]{2,1,0:T(8,128)(2,1)S(1)}, bf16[8,128,512]{2,1,0:T(8,128)(2,1)}, u32[]{:S(2)}, u32[]{:S(2)}) %collective-permute-start.21) | collective-permute-done | bytes 1048608 | tf_op jit(solution)/shard_map/ppermute | solution.py:408
  162.4 9.9 %collective-permute-done.24.refs_2_ = bf16[8,128,512]{2,1,0:T(8,128)(2,1)S(1)} collective-permute-done((bf16[8,128,512]{2,1,0:T(8,128)(2,1)S(1)}, bf16[8,128,512]{2,1,0:T(8,128)(2,1)S(1)}, u32[]{:S(2)}, u32[]{:S(2)}) %collective-permute-start.24) | collective-permute-done | bytes 1048608 | tf_op jit(solution)/shard_map/ppermute | solution.py:408
  177.1 6.7 %collective-permute-done.27.refs_2_ = bf16[8,128,512]{2,1,0:T(8,128)(2,1)} collective-permute-done((bf16[8,128,512]{2,1,0:T(8,128)(2,1)}, bf16[8,128,512]{2,1,0:T(8,128)(2,1)}, u32[]{:S(2)}, u32[]{:S(2)}) %collective-permute-start.27) | collective-permute-done | bytes 1048608 | tf_op jit(solution)/shard_map/ppermute | solution.py:408
  186.1 9.0 %collective-permute-done.30.refs_2_ = bf16[8,128,512]{2,1,0:T(8,128)(2,1)} collective-permute-done((bf16[8,128,512]{2,1,0:T(8,128)(2,1)}, bf16[8,128,512]{2,1,0:T(8,128)(2,1)}, u32[]{:S(2)}, u32[]{:S(2)}) %collective-permute-start.30) | collective-permute-done | bytes 1048608 | tf_op jit(solution)/shard_map/ppermute | solution.py:408
  201.9 10.5 %correlate.7 = (bf16[64,512,1024]{2,1,0:T(8,128)(2,1)}, s32[8,128]{1,0:T(8,128)}) custom-call(s32[3,4]{1,0:T(4,128)} %pad_add_fusion.offset_ref, f32[4,8]{1,0:T(4,128)} %multiply_bitcast_fusion.scale_ref, bf16[8,128,512]{2,1,0:T(8,128)(2,1)} %copy-done.7, bf16[8,128,512]{2,1,0:T(8,128)(2,1)} %copy-done.6, bf16[8,128,512]{2,1,0:T(8,128)(2,1)} %copy-done.5, ...), custom_call_target="tpu_custom_call" | custom-call | bytes 1024 | tf_op jit(solution)/shard_map/correlate/pallas_call | solution.py:358
  212.4 10.5 %correlate.8 = (bf16[64,512,1024]{2,1,0:T(8,128)(2,1)}, s32[8,128]{1,0:T(8,128)}) custom-call(s32[3,4]{1,0:T(4,128)} %pad_add_fusion.offset_ref, f32[4,8]{1,0:T(4,128)} %multiply_bitcast_fusion.scale_ref, bf16[8,128,512]{2,1,0:T(8,128)(2,1)} %get-tuple-element.41.refs_0_.refs_4_, ...), custom_call_target="tpu_custom_call", output_to_operand_aliasing={{0}: (16, {})} | custom-call | bytes 1024 | tf_op jit(solution)/shard_map/correlate/pallas_call | solution.py:358
  252.2 15.0 %correlate.9 = (bf16[64,512,1024]{2,1,0:T(8,128)(2,1)}, s32[8,128]{1,0:T(8,128)}) custom-call(s32[3,4]{1,0:T(4,128)} %pad_add_fusion.offset_ref, f32[4,8]{1,0:T(4,128)} %multiply_bitcast_fusion.scale_ref, bf16[8,128,512]{2,1,0:T(8,128)(2,1)} %get-tuple-element.41.refs_0_.refs_4_, ...), custom_call_target="tpu_custom_call", output_to_operand_aliasing={{0}: (20, {})} | custom-call | bytes 1024 | tf_op jit(solution)/shard_map/correlate/pallas_call | solution.py:358
  274.8 12.4 %collective-permute-done.37.refs_1_ = bf16[8,128,512]{2,1,0:T(8,128)(2,1)} collective-permute-done((bf16[8,128,512]{2,1,0:T(8,128)(2,1)}, bf16[8,128,512]{2,1,0:T(8,128)(2,1)}, u32[]{:S(2)}, u32[]{:S(2)}) %collective-permute-start.37) | collective-permute-done | bytes 1048608 | tf_op jit(solution)/shard_map/ppermute | solution.py:408
  291.9 6.3 %collective-permute-done.40.refs_2_ = bf16[8,128,512]{2,1,0:T(8,128)(2,1)} collective-permute-done((bf16[8,128,512]{2,1,0:T(8,128)(2,1)S(1)}, bf16[8,128,512]{2,1,0:T(8,128)(2,1)}, u32[]{:S(2)}, u32[]{:S(2)}) %collective-permute-start.40) | collective-permute-done | bytes 1048608 | tf_op jit(solution)/shard_map/ppermute | solution.py:408
  301.8 12.0 %collective-permute-done.38.refs_1_ = bf16[8,128,512]{2,1,0:T(8,128)(2,1)S(1)} collective-permute-done((bf16[8,128,512]{2,1,0:T(8,128)(2,1)S(1)}, bf16[8,128,512]{2,1,0:T(8,128)(2,1)S(1)}, u32[]{:S(2)}, u32[]{:S(2)}) %collective-permute-start.38) | collective-permute-done | bytes 1048608 | tf_op jit(solution)/shard_map/ppermute | solution.py:408
  317.1 14.9 %correlate.10 = (bf16[64,512,1024]{2,1,0:T(8,128)(2,1)}, s32[8,128]{1,0:T(8,128)}) custom-call(s32[3,4]{1,0:T(4,128)} %pad_add_fusion.offset_ref, f32[4,8]{1,0:T(4,128)} %multiply_bitcast_fusion.scale_ref, bf16[8,128,512]{2,1,0:T(8,128)(2,1)} %pick.32.refs_2_.refs_0_.refs_8_, ...), custom_call_target="tpu_custom_call", output_to_operand_aliasing={{0}: (24, {})} | custom-call | bytes 1024 | tf_op jit(solution)/shard_map/correlate/pallas_call | solution.py:358
  363.7 7.6 %collective-permute-done.48.refs_3_ = bf16[8,128,512]{2,1,0:T(8,128)(2,1)S(1)} collective-permute-done((bf16[8,128,512]{2,1,0:T(8,128)(2,1)}, bf16[8,128,512]{2,1,0:T(8,128)(2,1)S(1)}, u32[]{:S(2)}, u32[]{:S(2)}) %collective-permute-start.48) | collective-permute-done | bytes 1048608 | tf_op jit(solution)/shard_map/ppermute | solution.py:408
  389.6 4.7 collective-permute-done.57.refs_3_
  394.2 5.1 %collective-permute-start.62 = (bf16[8,128,512]{2,1,0:T(8,128)(2,1)S(1)}, bf16[8,128,512]{2,1,0:T(8,128)(2,1)}, u32[]{:S(2)}, u32[]{:S(2)}) collective-permute-start(bf16[8,128,512]{2,1,0:T(8,128)(2,1)S(1)} %copy-done.19), channel_id=1, source_target_pairs={{0,4},{1,5},{2,6},{3,7},{4,0},{5,1},{6,2},{7,3},{8,12},{9,13},{10,... | collective-permute-start | bytes 3145736 | tf_op jit(solution)/shard_map/ppermute | solution.py:408
  405.3 8.9 %collective-permute-done.66.refs_2_ = bf16[8,128,512]{2,1,0:T(8,128)(2,1)} collective-permute-done((bf16[8,128,512]{2,1,0:T(8,128)(2,1)S(1)}, bf16[8,128,512]{2,1,0:T(8,128)(2,1)}, u32[]{:S(2)}, u32[]{:S(2)}) %collective-permute-start.66) | collective-permute-done | bytes 1048608 | tf_op jit(solution)/shard_map/ppermute | solution.py:408
  421.2 19.3 %correlate.11 = (bf16[64,512,1024]{2,1,0:T(8,128)(2,1)}, s32[8,128]{1,0:T(8,128)}) custom-call(s32[3,4]{1,0:T(4,128)} %pad_add_fusion.offset_ref, f32[4,8]{1,0:T(4,128)} %multiply_bitcast_fusion.scale_ref, bf16[8,128,512]{2,1,0:T(8,128)(2,1)} %get-tuple-element.41.refs_0_.refs_4_, ...), custom_call_target="tpu_custom_call", output_to_operand_aliasing={{0}: (24, {})} | custom-call | bytes 1024 | tf_op jit(solution)/shard_map/correlate/pallas_call | solution.py:358
  443.7 19.3 %correlate.12 = (bf16[64,512,1024]{2,1,0:T(8,128)(2,1)}, s32[8,128]{1,0:T(8,128)}) custom-call(s32[3,4]{1,0:T(4,128)} %pad_add_fusion.offset_ref, f32[4,8]{1,0:T(4,128)} %multiply_bitcast_fusion.scale_ref, bf16[8,128,512]{2,1,0:T(8,128)(2,1)} %pick.36.refs_23_.refs_0_.refs_12_, ...), custom_call_target="tpu_custom_call", output_to_operand_aliasing={{0}: (32, {})} | custom-call | bytes 1024 | tf_op jit(solution)/shard_map/correlate/pallas_call | solution.py:358
  469.6 23.7 %correlate.13 = (bf16[64,512,1024]{2,1,0:T(8,128)(2,1)}, s32[8,128]{1,0:T(8,128)}) custom-call(s32[3,4]{1,0:T(4,128)} %pad_add_fusion.offset_ref, f32[4,8]{1,0:T(4,128)} %multiply_bitcast_fusion.scale_ref, bf16[8,128,512]{2,1,0:T(8,128)(2,1)} %get-tuple-element.41.refs_0_.refs_4_, ...), custom_call_target="tpu_custom_call", output_to_operand_aliasing={{0}: (28, {})} | custom-call | bytes 1024 | tf_op jit(solution)/shard_map/correlate/pallas_call | solution.py:358
  (275 shorter events, 189.9 us)
Async XLA Ops:
  11.8 100.2 %collective-permute-start = (bf16[32,128,512]{2,1,0:T(8,128)(2,1)}, bf16[32,128,512]{2,1,0:T(8,128)(2,1)}, u32[]{:S(2)}, u32[]{:S(2)}) collective-permute-start(bf16[32,128,512]{2,1,0:T(8,128)(2,1)} %get-tuple-element.45), channel_id=1, source_target_pairs={{0,1},{1,0},{2,3},{3,2},{4,5},{5,4},{6,7},{7,6},{8,9},{9,8},{10,11... | collective-permute-start | bytes 12582920 | tf_op jit(solution)/shard_map/ppermute | solution.py:408
  13.2 98.9 %collective-permute-start.1 = (bf16[32,128,512]{2,1,0:T(8,128)(2,1)}, bf16[32,128,512]{2,1,0:T(8,128)(2,1)}, u32[]{:S(2)}, u32[]{:S(2)}) collective-permute-start(bf16[32,128,512]{2,1,0:T(8,128)(2,1)} %get-tuple-element.45), channel_id=1, source_target_pairs={{1,2},{2,1},{5,6},{6,5},{9,10},{10,9},{13,14},{14,13},{17,18},{18,... | collective-permute-start | bytes 12582920 | tf_op jit(solution)/shard_map/ppermute | solution.py:408
  16.6 34.5 %collective-permute-start.3 = (bf16[8,128,512]{2,1,0:T(8,128)(2,1)S(1)}, bf16[8,128,512]{2,1,0:T(8,128)(2,1)S(1)}, u32[]{:S(2)}, u32[]{:S(2)}) collective-permute-start(bf16[8,128,512]{2,1,0:T(8,128)(2,1)S(1)} %collective-permute-done.2.refs_1_), channel_id=1, source_target_pairs={{8,24},{20,28},{25,17},{5,21},{2,10},{30,14},{19,3},{15,7}} | collective-permute-start | bytes 3145736 | tf_op jit(solution)/shard_map/ppermute | solution.py:408
  17.9 44.4 %collective-permute-start.6 = (bf16[8,128,512]{2,1,0:T(8,128)(2,1)S(1)}, bf16[8,128,512]{2,1,0:T(8,128)(2,1)}, u32[]{:S(2)}, u32[]{:S(2)}) collective-permute-start(bf16[8,128,512]{2,1,0:T(8,128)(2,1)S(1)} %collective-permute-done.5.refs_1_), channel_id=1, source_target_pairs={{8,24},{20,28},{25,17},{5,21},{2,10},{30,14},{19,3},{15,7}} | collective-permute-start | bytes 3145736 | tf_op jit(solution)/shard_map/ppermute | solution.py:408
  19.2 54.3 %collective-permute-start.9 = (bf16[8,128,512]{2,1,0:T(8,128)(2,1)S(1)}, bf16[8,128,512]{2,1,0:T(8,128)(2,1)}, u32[]{:S(2)}, u32[]{:S(2)}) collective-permute-start(bf16[8,128,512]{2,1,0:T(8,128)(2,1)S(1)} %collective-permute-done.8.refs_1_), channel_id=1, source_target_pairs={{8,24},{20,28},{25,17},{5,21},{2,10},{30,14},{19,3},{15,7}} | collective-permute-start | bytes 3145736 | tf_op jit(solution)/shard_map/ppermute | solution.py:408
  51.1 33.7 %collective-permute-start.12 = (bf16[8,128,512]{2,1,0:T(8,128)(2,1)S(1)}, bf16[8,128,512]{2,1,0:T(8,128)(2,1)}, u32[]{:S(2)}, u32[]{:S(2)}) collective-permute-start(bf16[8,128,512]{2,1,0:T(8,128)(2,1)S(1)} %collective-permute-done.11.refs_1_), channel_id=1, source_target_pairs={{8,24},{20,28},{25,17},{5,21},{2,10},{30,14},{19,3},{15,7}} | collective-permute-start | bytes 3145736 | tf_op jit(solution)/shard_map/ppermute | solution.py:408
  121.5 112.2 %collective-permute-start.14 = (bf16[32,128,512]{2,1,0:T(8,128)(2,1)}, bf16[32,128,512]{2,1,0:T(8,128)(2,1)}, u32[]{:S(2)}, u32[]{:S(2)}) collective-permute-start(bf16[32,128,512]{2,1,0:T(8,128)(2,1)} %collective-permute-done.1.refs_0_), channel_id=1, source_target_pairs={{1,0},{2,3},{5,4},{6,7},{9,8},{10,11},{13,12},{14,15},{17,16},{18,... | collective-permute-start | bytes 12582920 | tf_op jit(solution)/shard_map/ppermute | solution.py:408
  122.8 110.9 %collective-permute-start.15 = (bf16[32,128,512]{2,1,0:T(8,128)(2,1)}, bf16[32,128,512]{2,1,0:T(8,128)(2,1)}, u32[]{:S(2)}, u32[]{:S(2)}) collective-permute-start(bf16[32,128,512]{2,1,0:T(8,128)(2,1)} %collective-permute-done), channel_id=1, source_target_pairs={{1,2},{2,1},{5,6},{6,5},{9,10},{10,9},{13,14},{14,13},{17,18},{18,... | collective-permute-start | bytes 12582920 | tf_op jit(solution)/shard_map/ppermute | solution.py:408
  127.2 33.9 %collective-permute-start.21 = (bf16[8,128,512]{2,1,0:T(8,128)(2,1)S(1)}, bf16[8,128,512]{2,1,0:T(8,128)(2,1)}, u32[]{:S(2)}, u32[]{:S(2)}) collective-permute-start(bf16[8,128,512]{2,1,0:T(8,128)(2,1)S(1)} %collective-permute-done.20.refs_1_), channel_id=1, source_target_pairs={{8,24},{20,28},{25,17},{5,21},{2,10},{30,14},{19,3},{15,7}} | collective-permute-start | bytes 3145736 | tf_op jit(solution)/shard_map/ppermute | solution.py:408
  128.5 43.8 %collective-permute-start.24 = (bf16[8,128,512]{2,1,0:T(8,128)(2,1)S(1)}, bf16[8,128,512]{2,1,0:T(8,128)(2,1)S(1)}, u32[]{:S(2)}, u32[]{:S(2)}) collective-permute-start(bf16[8,128,512]{2,1,0:T(8,128)(2,1)S(1)} %collective-permute-done.23.refs_1_), channel_id=1, source_target_pairs={{8,24},{20,28},{25,17},{5,21},{2,10},{30,14},{19,3},{15,7}} | collective-permute-start | bytes 3145736 | tf_op jit(solution)/shard_map/ppermute | solution.py:408
  129.8 54.0 %collective-permute-start.27 = (bf16[8,128,512]{2,1,0:T(8,128)(2,1)}, bf16[8,128,512]{2,1,0:T(8,128)(2,1)}, u32[]{:S(2)}, u32[]{:S(2)}) collective-permute-start(bf16[8,128,512]{2,1,0:T(8,128)(2,1)} %collective-permute-done.26.refs_1_), channel_id=1, source_target_pairs={{8,24},{20,28},{25,17},{5,21},{2,10},{30,14},{19,3},{15,7}} | collective-permute-start | bytes 3145736 | tf_op jit(solution)/shard_map/ppermute | solution.py:408
  161.1 33.9 %collective-permute-start.30 = (bf16[8,128,512]{2,1,0:T(8,128)(2,1)}, bf16[8,128,512]{2,1,0:T(8,128)(2,1)}, u32[]{:S(2)}, u32[]{:S(2)}) collective-permute-start(bf16[8,128,512]{2,1,0:T(8,128)(2,1)} %collective-permute-done.29.refs_1_), channel_id=1, source_target_pairs={{8,24},{20,28},{25,17},{5,21},{2,10},{30,14},{19,3},{15,7}} | collective-permute-start | bytes 3145736 | tf_op jit(solution)/shard_map/ppermute | solution.py:408
  183.8 41.8 %collective-permute-start.25 = (bf16[8,128,512]{2,1,0:T(8,128)(2,1)}, bf16[8,128,512]{2,1,0:T(8,128)(2,1)}, u32[]{:S(2)}, u32[]{:S(2)}) collective-permute-start(bf16[8,128,512]{2,1,0:T(8,128)(2,1)} %copy-done.29), channel_id=1, source_target_pairs={{24,16},{28,12},{17,1},{21,29},{10,26},{14,6},{3,11},{7,23}} | collective-permute-start | bytes 3145736 | tf_op jit(solution)/shard_map/ppermute | solution.py:408
  247.9 39.3 %collective-permute-start.37 = (bf16[8,128,512]{2,1,0:T(8,128)(2,1)}, bf16[8,128,512]{2,1,0:T(8,128)(2,1)}, u32[]{:S(2)}, u32[]{:S(2)}) collective-permute-start(bf16[8,128,512]{2,1,0:T(8,128)(2,1)} %get-tuple-element.77), channel_id=1, source_target_pairs={{1,0},{2,3},{5,4},{6,7},{9,8},{10,11},{13,12},{14,15},{17,16},{18,... | collective-permute-start | bytes 3145736 | tf_op jit(solution)/shard_map/ppermute | solution.py:408
  249.2 38.7 %collective-permute-start.52 = (bf16[8,128,512]{2,1,0:T(8,128)(2,1)}, bf16[8,128,512]{2,1,0:T(8,128)(2,1)S(1)}, u32[]{:S(2)}, u32[]{:S(2)}) collective-permute-start(bf16[8,128,512]{2,1,0:T(8,128)(2,1)} %pick.34.refs_2_.refs_0_.refs_10_), channel_id=1, source_target_pairs={{0,8},{4,20},{9,25},{13,5},{18,2},{22,30},{27,19},{31,15}} | collective-permute-start | bytes 3145736 | tf_op jit(solution)/shard_map/ppermute | solution.py:408
  289.3 44.8 %collective-permute-start.53 = (bf16[8,128,512]{2,1,0:T(8,128)(2,1)S(1)}, bf16[8,128,512]{2,1,0:T(8,128)(2,1)S(1)}, u32[]{:S(2)}, u32[]{:S(2)}) collective-permute-start(bf16[8,128,512]{2,1,0:T(8,128)(2,1)S(1)} %collective-permute-done.52.refs_1_), channel_id=1, source_target_pairs={{8,24},{20,28},{25,17},{5,21},{2,10},{30,14},{19,3},{15,7}} | collective-permute-start | bytes 3145736 | tf_op jit(solution)/shard_map/ppermute | solution.py:408
  290.6 45.1 %collective-permute-start.50 = (bf16[8,128,512]{2,1,0:T(8,128)(2,1)}, bf16[8,128,512]{2,1,0:T(8,128)(2,1)}, u32[]{:S(2)}, u32[]{:S(2)}) collective-permute-start(bf16[8,128,512]{2,1,0:T(8,128)(2,1)} %collective-permute-done.49.refs_1_), channel_id=1, source_target_pairs={{8,24},{20,28},{25,17},{5,21},{2,10},{30,14},{19,3},{15,7}} | collective-permute-start | bytes 3145736 | tf_op jit(solution)/shard_map/ppermute | solution.py:408
  298.2 41.1 %collective-permute-start.44 = (bf16[8,128,512]{2,1,0:T(8,128)(2,1)S(1)}, bf16[8,128,512]{2,1,0:T(8,128)(2,1)}, u32[]{:S(2)}, u32[]{:S(2)}) collective-permute-start(bf16[8,128,512]{2,1,0:T(8,128)(2,1)S(1)} %collective-permute-done.43.refs_2_), channel_id=1, source_target_pairs={{24,16},{28,12},{17,1},{21,29},{10,26},{14,6},{3,11},{7,23}} | collective-permute-start | bytes 3145736 | tf_op jit(solution)/shard_map/ppermute | solution.py:408
  300.5 40.2 %collective-permute-start.47 = (bf16[8,128,512]{2,1,0:T(8,128)(2,1)S(1)}, bf16[8,128,512]{2,1,0:T(8,128)(2,1)}, u32[]{:S(2)}, u32[]{:S(2)}) collective-permute-start(bf16[8,128,512]{2,1,0:T(8,128)(2,1)S(1)} %collective-permute-done.46.refs_1_), channel_id=1, source_target_pairs={{8,24},{20,28},{25,17},{5,21},{2,10},{30,14},{19,3},{15,7}} | collective-permute-start | bytes 3145736 | tf_op jit(solution)/shard_map/ppermute | solution.py:408
  352.1 34.8 %collective-permute-start.58 = (bf16[8,128,512]{2,1,0:T(8,128)(2,1)}, bf16[8,128,512]{2,1,0:T(8,128)(2,1)}, u32[]{:S(2)}, u32[]{:S(2)}) collective-permute-start(bf16[8,128,512]{2,1,0:T(8,128)(2,1)} %pick.40.refs_4_.refs_0_.refs_2_.refs_14_), channel_id=1, source_target_pairs={{0,8},{4,20},{9,25},{13,5},{18,2},{22,30},{27,19},{31,15}} | collective-permute-start | bytes 3145736 | tf_op jit(solution)/shard_map/ppermute | solution.py:408
  403.0 37.5 %collective-permute-start.60 = (bf16[8,128,512]{2,1,0:T(8,128)(2,1)}, bf16[8,128,512]{2,1,0:T(8,128)(2,1)}, u32[]{:S(2)}, u32[]{:S(2)}) collective-permute-start(bf16[8,128,512]{2,1,0:T(8,128)(2,1)} %collective-permute-done.59.refs_2_), channel_id=1, source_target_pairs={{24,16},{28,12},{17,1},{21,29},{10,26},{14,6},{3,11},{7,23}} | collective-permute-start | bytes 3145736 | tf_op jit(solution)/shard_map/ppermute | solution.py:408
  414.2 48.8 %collective-permute-start.67 = (bf16[8,128,512]{2,1,0:T(8,128)(2,1)}, bf16[8,128,512]{2,1,0:T(8,128)(2,1)}, u32[]{:S(2)}, u32[]{:S(2)}) collective-permute-start(bf16[8,128,512]{2,1,0:T(8,128)(2,1)} %collective-permute-done.66.refs_2_), channel_id=1, source_target_pairs={{24,16},{28,12},{17,1},{21,29},{10,26},{14,6},{3,11},{7,23}} | collective-permute-start | bytes 3145736 | tf_op jit(solution)/shard_map/ppermute | solution.py:408
  419.2 46.6 %collective-permute-start.68 = (bf16[8,128,512]{2,1,0:T(8,128)(2,1)S(1)}, bf16[8,128,512]{2,1,0:T(8,128)(2,1)S(1)}, u32[]{:S(2)}, u32[]{:S(2)}) collective-permute-start(bf16[8,128,512]{2,1,0:T(8,128)(2,1)S(1)} %copy-done.21), channel_id=1, source_target_pairs={{0,4},{1,5},{2,6},{3,7},{4,0},{5,1},{6,2},{7,3},{8,12},{9,13},{10,... | collective-permute-start | bytes 3145736 | tf_op jit(solution)/shard_map/ppermute | solution.py:408
  420.2 45.6 %collective-permute-start.69 = (bf16[8,128,512]{2,1,0:T(8,128)(2,1)}, bf16[8,128,512]{2,1,0:T(8,128)(2,1)S(1)}, u32[]{:S(2)}, u32[]{:S(2)}) collective-permute-start(bf16[8,128,512]{2,1,0:T(8,128)(2,1)} %pick.45.refs_23_.refs_17_), channel_id=1, source_target_pairs={{0,4},{1,5},{2,6},{3,7},{4,0},{5,1},{6,2},{7,3},{8,12},{9,13},{10,... | collective-permute-start | bytes 3145736 | tf_op jit(solution)/shard_map/ppermute | solution.py:408
  (97 other events, 2106.5 us)
